TPU v7x, 512 devices: a whole 4x4x16 slice. The times are simulated.
512 devices in a mesh: lon: 32 (over x_lo, z), lat: 16 (over y, x_hi, core).
Axes of the slice: x: 4 (x_hi: 2, x_lo: 2; x = x_hi * 2 + x_lo), y: 4, z: 16, core: 2. Of those that a mesh axis runs over, the one named last changes fastest.
Arguments:
- potential_warmth: float32 [32, 512, 4096], P(None, 'lat', 'lon'), may hold values from -2 to 30
- practical_saltiness: float32 [32, 512, 4096], P(None, 'lat', 'lon'), may hold values from 33 to 37
- zonal_velocity_array: float32 [32, 512, 4096], P(None, 'lat', 'lon'), may hold values from -3 to 3
- meridional_velocity_array: float32 [32, 512, 4096], P(None, 'lat', 'lon'), may hold values from -3 to 3
- interface_diffusion_number: float32 [32, 512, 4096], P(None, 'lat', 'lon'), may hold values from 0.05 to 5
- open_water_indicator: int32 [32, 512, 4096], P(None, 'lat', 'lon'), may hold values from 0 to 1, as said below
- bottom_layer_index: int32 [512, 4096], P('lat', 'lon'), may hold values from 0 to 32, as said below
Outputs:
- temperature_next: float32 [32, 512, 4096], P(None, 'lat', 'lon')
- salinity_next: float32 [32, 512, 4096], P(None, 'lat', 'lon')
- zonal_next: float32 [32, 512, 4096], P(None, 'lat', 'lon')
- meridional_next: float32 [32, 512, 4096], P(None, 'lat', 'lon')
Inputs may be any that keep to these rules, and one draw needn't show every extreme that they name: bottom_layer_index counts the wet levels of a column from the surface; open_water_indicator is 0 at every level k >= bottom_layer_index of the column; some column reaches 32 levels and some column has none. `open_water_indicator`: above the sea floor at most the top two levels of a column are closed.
All inputs are finite; a program needn't handle non-finite values.
Results may differ from a plain program's by a relative error of at most 0.00002.
Values sent between devices are 32-bit elements; how exact they have to be, the bound alone decides.
A program may use at most 64 MiB of HBM per device.

v0:
```python
import functools
import math

import jax
import jax.numpy as jnp
from jax import lax
from jax.experimental import pallas as pl
from jax.experimental.pallas import tpu as pltpu
from jax.sharding import PartitionSpec as P

THERMAL_EXPAND = 0.1655
HALINE_CONTRACT = 0.76554
THERMAL_CABBELING = 0.05952
HALINE_CABBELING = 0.00074914
THERMAL_PRESSURE = 0.0001497
HALINE_PRESSURE = 1.109e-05
MIXED_CABBELING = 0.0024341
ADVECT = 0.2
DIFFUSE = 0.08
VISCOUS = 0.08
GRADIENT = 0.1
ROTATION = 0.25
BOTTOM_DRAG = 1.0
OCEAN_DEPTH = 4000.0

MESH = pl.DeviceIdType.MESH
LEVELS = 32
ROWS = 32
LANES = 128
CELLS = LEVELS * ROWS
FIELDS = 4
MASK_ROW = FIELDS * LEVELS
PRESSURE_SCALE = 0.5 / LEVELS * (0.5 * GRADIENT / VISCOUS)
FACE = 0.25 * ADVECT / DIFFUSE


def half_density(warm, salt, wet, level):
    thermal = warm - 10.0
    haline = salt - 35.0
    depth = (level + 0.5) * (OCEAN_DEPTH / LEVELS)
    s = PRESSURE_SCALE
    by_thermal = -THERMAL_EXPAND * s - (THERMAL_EXPAND * THERMAL_PRESSURE * s) * depth
    by_haline = HALINE_CONTRACT * s - (HALINE_CONTRACT * HALINE_PRESSURE * s) * depth
    value = thermal * (
        by_thermal
        - (0.5 * THERMAL_EXPAND * THERMAL_CABBELING * s) * thermal
        - (MIXED_CABBELING * s) * haline
    ) + haline * (by_haline - (0.5 * HALINE_CONTRACT * HALINE_CABBELING * s) * haline)
    return jnp.where(wet, value, 0.0)


def inverse(x):
    r = pl.reciprocal(x, approx=True)
    return r * (2.0 - x * r)


def iota(axis):
    return lax.broadcasted_iota(jnp.int32, (ROWS, LANES), axis)


def kernel(
    lat_count,
    lon_count,
    warm_hbm,
    salt_hbm,
    zonal_hbm,
    merid_hbm,
    mixing_hbm,
    open_hbm,
    bottom_hbm,
    warm_out,
    salt_out,
    zonal_out,
    merid_out,
    warm,
    salt,
    zonal,
    merid,
    mixing,
    top_open,
    bottom,
    stars,
    link,
    inv_tracer,
    inv_momentum,
    row_send,
    row_recv,
    col_send,
    col_recv,
    col_fix,
    load_sem,
    send_sem,
    recv_sem,
):
    lat = lax.axis_index("lat")
    lon = lax.axis_index("lon")
    is_south = lat == 0
    is_north = lat == lat_count - 1
    east = {"lon": lax.rem(lon + 1, lon_count)}
    west = {"lon": lax.rem(lon + lon_count - 1, lon_count)}
    south = {"lat": jnp.maximum(lat - 1, 0)}
    north_lat = jnp.minimum(lat + 1, lat_count - 1)
    north_lon = jnp.where(is_north, lon_count - 1 - lon, lon)
    north = {"lat": north_lat, "lon": north_lon}

    loads = [
        pltpu.make_async_copy(src, dst, load_sem.at[n])
        for n, (src, dst) in enumerate(
            (
                (bottom_hbm, bottom),
                (open_hbm.at[pl.ds(0, 2 * ROWS)], top_open),
                (warm_hbm, warm.at[pl.ds(0, CELLS)]),
                (salt_hbm, salt.at[pl.ds(0, CELLS)]),
                (zonal_hbm, zonal.at[pl.ds(0, CELLS)]),
                (merid_hbm, merid.at[pl.ds(0, CELLS)]),
                (mixing_hbm, mixing),
            )
        )
    ]
    for load in loads:
        load.start()

    barrier = pltpu.get_barrier_semaphore()
    for target in (east, west, north):
        pl.semaphore_signal(barrier, inc=1, device_id=target, device_id_type=MESH)

    @pl.when(lat > 0)
    def _():
        pl.semaphore_signal(barrier, inc=1, device_id=south, device_id_type=MESH)

    fields = (warm, salt, zonal, merid)
    lane = iota(1)
    row = iota(0)
    for field in fields:
        field[pl.ds(CELLS, 8)] = jnp.zeros((8, LANES), jnp.float32)

    @pl.when(is_south)
    def _():
        row_recv[0] = jnp.zeros((MASK_ROW + 8, LANES), jnp.float32)

    row_global = (lat * ROWS + row).astype(jnp.float32)
    coriolis = ROTATION * jnp.sin(
        math.pi / 180.0 * (-80.0 + 170.0 * (row_global + 0.5) / (ROWS * lat_count))
    )

    for load in loads:
        load.wait()

    deep = bottom[...].astype(jnp.float32)
    open0 = top_open[pl.ds(0, ROWS)].astype(jnp.float32)
    open1 = top_open[pl.ds(ROWS, ROWS)].astype(jnp.float32)
    for side, edge in ((0, 0), (1, ROWS - 1)):
        for n, field in enumerate(fields):
            row_send[side, pl.ds(n * LEVELS, LEVELS)] = field[pl.ds(edge, LEVELS, stride=ROWS)]
        for n, plane in enumerate((deep, open0, open1)):
            row_send[side, pl.ds(MASK_ROW + n, 1)] = plane[edge : edge + 1]
        row_send[side, pl.ds(MASK_ROW + 3, 5)] = jnp.zeros((5, LANES), jnp.float32)

    @pl.when(is_north)
    def _():
        flip = (LANES - 1) - lax.broadcasted_iota(jnp.int32, (8, LANES), 1)
        for tile in range((MASK_ROW + 8) // 8):
            there = pl.ds(tile * 8, 8)
            turned = jnp.take_along_axis(row_send[1, there], flip, axis=1)
            if 2 * LEVELS <= tile * 8 < 4 * LEVELS:
                turned = -turned
            row_send[1, there] = turned

    pl.semaphore_wait(barrier, jnp.where(is_south, 3, 4))

    to_north = pltpu.make_async_remote_copy(
        src_ref=row_send.at[1],
        dst_ref=row_recv.at[jnp.where(is_north, 1, 0)],
        send_sem=send_sem.at[1],
        recv_sem=recv_sem.at[jnp.where(is_north, 1, 0)],
        device_id=north,
        device_id_type=MESH,
    )
    to_north.start()
    to_south = pltpu.make_async_remote_copy(
        src_ref=row_send.at[0],
        dst_ref=row_recv.at[1],
        send_sem=send_sem.at[0],
        recv_sem=recv_sem.at[1],
        device_id=south,
        device_id_type=MESH,
    )

    @pl.when(lat > 0)
    def _():
        to_south.start()

    def pack(k, sums):
        easts, wests = sums
        for n, field in enumerate(fields):
            at = n * LEVELS + k
            turned = pltpu.roll(field[pl.ds(pl.multiple_of(k * ROWS, ROWS), ROWS)], at + 1, axis=1)
            easts = jnp.where(lane == at, turned, easts)
            wests = jnp.where(lane == lax.rem(at + 1, LANES), turned, wests)
        return easts, wests

    nothing = jnp.zeros((ROWS, LANES), jnp.float32)
    easts, wests = lax.fori_loop(0, LEVELS, pack, (nothing, nothing), unroll=4)
    col_send[1, pl.ds(0, ROWS)] = easts
    col_send[0, pl.ds(0, ROWS)] = wests
    east_masks = nothing
    west_masks = nothing
    for n, plane in enumerate((deep, open0, open1)):
        turned = pltpu.roll(plane, n + 1, axis=1)
        east_masks = jnp.where(lane == n, turned, east_masks)
        west_masks = jnp.where(lane == n + 1, turned, west_masks)
    col_send[1, pl.ds(ROWS, ROWS)] = east_masks
    col_send[0, pl.ds(ROWS, ROWS)] = west_masks
    to_east = pltpu.make_async_remote_copy(
        src_ref=col_send.at[1],
        dst_ref=col_recv.at[0],
        send_sem=send_sem.at[3],
        recv_sem=recv_sem.at[2],
        device_id=east,
        device_id_type=MESH,
    )
    to_west = pltpu.make_async_remote_copy(
        src_ref=col_send.at[0],
        dst_ref=col_recv.at[1],
        send_sem=send_sem.at[2],
        recv_sem=recv_sem.at[3],
        device_id=west,
        device_id_type=MESH,
    )
    to_east.start()
    to_west.start()

    depth_here = bottom[...]
    not_east = lane < LANES - 1
    not_north = row < ROWS - 1
    depth_east = jnp.where(
        not_east, jnp.minimum(depth_here, pltpu.roll(depth_here, LANES - 1, axis=1)), 0
    )
    depth_north = jnp.where(
        not_north, jnp.minimum(depth_here, pltpu.roll(depth_here, ROWS - 1, axis=0)), 0
    )

    def level(k, masks, carried):
        above, g_above, pressure_sum = carried
        wet, wet_east, wet_north, wet_below = masks
        k_float = jnp.asarray(k, jnp.int32).astype(jnp.float32)
        start = k * ROWS
        here = pl.ds(start if isinstance(k, int) else pl.multiple_of(start, ROWS), ROWS)
        shifted = pl.ds(start + 1, ROWS)
        t, s, u, v = (field[here] for field in fields)
        t_n, s_n, u_n, v_n = (field[shifted] for field in fields)
        t_e, s_e, u_e, v_e = (pltpu.roll(x, LANES - 1, axis=1) for x in (t, s, u, v))

        half = half_density(t, s, wet, k_float)
        pressure = pressure_sum + half
        pressure_sum = pressure + half
        p_e = pltpu.roll(pressure, LANES - 1, axis=1)
        p_n = pltpu.roll(pressure, ROWS - 1, axis=0)

        a_e = FACE * (u + u_e)
        a_n = FACE * (v + v_n)
        ahead_e = jnp.where(wet_east, a_e - 1.0, 0.0)
        behind_e = jnp.where(wet_east, a_e + 1.0, 0.0)
        ahead_n = jnp.where(wet_north, a_n - 1.0, 0.0)
        behind_n = jnp.where(wet_north, a_n + 1.0, 0.0)

        def spread(f_e, f_n):
            return (f_e - pltpu.roll(f_e, 1, axis=1)) + (f_n - pltpu.roll(f_n, 1, axis=0))

        def tracer(q, q_e, q_n):
            f_e = ahead_e * q_e + behind_e * q
            f_n = ahead_n * q_n + behind_n * q
            return jnp.where(wet, q - DIFFUSE * spread(f_e, f_n), 0.0)

        stars[0, here] = tracer(t, t_e, t_n)
        stars[1, here] = tracer(s, s_e, s_n)

        du_e = jnp.where(wet_east, u_e - u, 0.0)
        dp_e = jnp.where(wet_east, p_e - pressure, 0.0)
        du_n = jnp.where(wet_north, u_n - u, 0.0)
        lap_u = ((du_e - dp_e) - pltpu.roll(du_e + dp_e, 1, axis=1)) + (
            du_n - pltpu.roll(du_n, 1, axis=0)
        )
        stars[2, here] = jnp.where(wet, u + VISCOUS * lap_u + coriolis * v, 0.0)
        dv_n = jnp.where(wet_north, v_n - v, 0.0)
        dp_n = jnp.where(wet_north, p_n - pressure, 0.0)
        dv_e = jnp.where(wet_east, v_e - v, 0.0)
        lap_v = ((dv_n - dp_n) - pltpu.roll(dv_n + dp_n, 1, axis=0)) + (
            dv_e - pltpu.roll(dv_e, 1, axis=1)
        )
        stars[3, here] = jnp.where(wet, v + VISCOUS * lap_v - coriolis * u, 0.0)

        below = jnp.where(wet_below, mixing[here], 0.0)
        diagonal = (1.0 + below) + above * (1.0 - g_above)
        inv = inverse(diagonal)
        dragged = jnp.logical_and(depth_here == k + 1, wet)
        inv_m = inverse(diagonal + jnp.where(dragged, BOTTOM_DRAG, 0.0))
        link[here] = below
        inv_tracer[here] = inv
        inv_momentum[here] = inv_m
        return below, below * inv, pressure_sum

    def open_pair(plane):
        wet = plane > 0.5
        wet_east = jnp.where(not_east, plane * pltpu.roll(plane, LANES - 1, axis=1), 0.0) > 0.5
        wet_north = jnp.where(not_north, plane * pltpu.roll(plane, ROWS - 1, axis=0), 0.0) > 0.5
        return wet, wet_east, wet_north

    carried = (nothing, nothing, nothing)
    carried = level(0, open_pair(open0) + (open0 * open1 > 0.5,), carried)
    carried = level(
        1,
        open_pair(open1) + (jnp.logical_and(open1 > 0.5, depth_here > 2),),
        carried,
    )

    def deeper(k, carried):
        masks = (depth_here > k, depth_east > k, depth_north > k, depth_here > k + 1)
        return level(k, masks, carried)

    lax.fori_loop(2, LEVELS, deeper, carried)

    pltpu.make_async_remote_copy(
        src_ref=row_send.at[1],
        dst_ref=row_recv.at[1],
        send_sem=send_sem.at[1],
        recv_sem=recv_sem.at[1],
        device_id=north,
        device_id_type=MESH,
    ).wait_recv()

    @pl.when(lat > 0)
    def _():
        pltpu.make_async_remote_copy(
            src_ref=row_send.at[0],
            dst_ref=row_recv.at[0],
            send_sem=send_sem.at[0],
            recv_sem=recv_sem.at[0],
            device_id=south,
            device_id_type=MESH,
        ).wait_recv()

    def wet_levels(level_index, depth, first, second):
        return jnp.where(
            level_index == 0,
            first,
            jnp.where(
                level_index == 1,
                second,
                jnp.where(level_index.astype(jnp.float32) < depth, 1.0, 0.0),
            ),
        )

    def summed(half, axis, index):
        total = half
        for step in (1, 2, 4, 8, 16):
            total = total + jnp.where(index >= step, pltpu.roll(total, step, axis=axis), 0.0)
        return 2.0 * total - half

    def edge_faces(q, q_o, a, face):
        return jnp.where(face, (a - 1.0) * q_o + (a + 1.0) * q, 0.0)

    for side, edge in ((0, 0), (1, ROWS - 1)):
        there = pl.ds(edge, LEVELS, stride=ROWS)
        own = [field[there] for field in fields]
        other = [row_recv[side, pl.ds(n * LEVELS, LEVELS)] for n in range(FIELDS)]
        own_wet = wet_levels(row, deep[edge : edge + 1], open0[edge : edge + 1], open1[edge : edge + 1])
        other_wet = wet_levels(
            row, *(row_recv[side, pl.ds(MASK_ROW + n, 1)] for n in range(3))
        )
        own_p = summed(half_density(own[0], own[1], own_wet > 0.5, row.astype(jnp.float32)), 0, row)
        other_p = summed(
            half_density(other[0], other[1], other_wet > 0.5, row.astype(jnp.float32)), 0, row
        )
        face = own_wet * other_wet > 0.5
        sign = 1.0 if side else -1.0
        a = (sign * FACE) * (own[3] + other[3])
        for n in (0, 1):
            stars[n, there] += -DIFFUSE * edge_faces(own[n], other[n], a, face)
        stars[2, there] += jnp.where(face, VISCOUS * (other[2] - own[2]), 0.0)
        stars[3, there] += jnp.where(
            face, VISCOUS * ((other[3] - own[3]) - sign * (other_p - own_p)), 0.0
        )

    for side, sem in ((0, 2), (1, 3)):
        pltpu.make_async_remote_copy(
            src_ref=col_send.at[side],
            dst_ref=col_recv.at[side],
            send_sem=send_sem.at[sem],
            recv_sem=recv_sem.at[sem],
            device_id=east,
            device_id_type=MESH,
        ).wait_recv()
    level_lane = lax.rem(lane, LEVELS)
    level_lane_float = level_lane.astype(jnp.float32)
    first_group = lane < LEVELS
    fixes = []
    for side in (0, 1):
        own = col_send[side, pl.ds(0, ROWS)]
        other = col_recv[side, pl.ds(0, ROWS)]
        own_mask = col_send[side, pl.ds(ROWS, ROWS)]
        other_mask = col_recv[side, pl.ds(ROWS, ROWS)]
        if side == 0:
            own = pltpu.roll(own, LANES - 1, axis=1)
            own_mask = pltpu.roll(own_mask, LANES - 1, axis=1)
        else:
            other = pltpu.roll(other, LANES - 1, axis=1)
            other_mask = pltpu.roll(other_mask, LANES - 1, axis=1)

        def spread_mask(mask):
            return wet_levels(
                level_lane,
                *(jnp.broadcast_to(mask[:, n : n + 1], (ROWS, LANES)) for n in range(3)),
            )

        own_wet = spread_mask(own_mask)
        other_wet = spread_mask(other_mask)

        def pressure_of(packed, wet):
            half = half_density(
                packed,
                pltpu.roll(packed, LANES - LEVELS, axis=1),
                jnp.logical_and(wet > 0.5, first_group),
                level_lane_float,
            )
            return summed(half, 1, lane)

        jump_p = pressure_of(other, other_wet) - pressure_of(own, own_wet)
        face = own_wet * other_wet > 0.5
        sign = 1.0 if side else -1.0
        both = own + other
        a = (sign * FACE) * jnp.where(
            first_group, pltpu.roll(both, 2 * LEVELS, axis=1), pltpu.roll(both, 3 * LEVELS, axis=1)
        )
        tracers = -DIFFUSE * edge_faces(own, other, a, face)
        jump = other - own
        jump = jnp.where(
            lane < 3 * LEVELS, jump - sign * pltpu.roll(jump_p, 2 * LEVELS, axis=1), jump
        )
        currents = jnp.where(face, VISCOUS * jump, 0.0)
        fixes.append(jnp.where(lane < 2 * LEVELS, tracers, currents))
    west_fix = pltpu.roll(fixes[0], 1, axis=1)
    east_fix = fixes[1]
    even_lane = lax.rem(lane, 2) == 0
    col_fix[0] = jnp.where(even_lane, east_fix, west_fix)
    col_fix[1] = jnp.where(even_lane, west_fix, east_fix)

    edge_lane = jnp.logical_or(lane == 0, lane == LANES - 1)

    def forward(k, carried):
        above, *values = carried
        here = pl.ds(pl.multiple_of(k * ROWS, ROWS), ROWS)
        fix = col_fix[lax.rem(k, 2)]
        invs = (inv_tracer[here], inv_momentum[here])
        new = []
        for n in range(FIELDS):
            turned = pltpu.roll(fix, LANES - 1 - n * LEVELS - k, axis=1)
            star = stars[n, here] + jnp.where(edge_lane, turned, 0.0)
            value = (star + above * values[n]) * invs[n // 2]
            stars[n, here] = value
            new.append(value)
        return (link[here], *new)

    _, *values = lax.fori_loop(0, LEVELS, forward, (nothing,) * 5)

    outs = (warm_out, salt_out, zonal_out, merid_out)
    last = pl.ds(CELLS - ROWS, ROWS)
    for n in range(FIELDS):
        outs[n][last] = values[n]

    def backward(step, values):
        k = LEVELS - 2 - step
        here = pl.ds(pl.multiple_of(k * ROWS, ROWS), ROWS)
        ratio = link[here] * inv_tracer[here]
        new = []
        for n in range(FIELDS):
            value = stars[n, here] + ratio * values[n]
            outs[n][here] = value
            new.append(value)
        return tuple(new)

    lax.fori_loop(0, LEVELS - 1, backward, tuple(values))

    to_north.wait_send()
    to_east.wait_send()
    to_west.wait_send()

    @pl.when(lat > 0)
    def _():
        to_south.wait_send()


def solution(mesh):
    lat_count = mesh.shape["lat"]
    lon_count = mesh.shape["lon"]

    def step(warm, salt, zonal, merid, mixing, open_water, bottom):
        flat = [x.reshape(CELLS, LANES) for x in (warm, salt, zonal, merid, mixing, open_water)]
        f32 = jnp.float32
        outs = pl.pallas_call(
            functools.partial(kernel, lat_count, lon_count),
            out_shape=[pltpu.VMEM((CELLS, LANES), f32)] * FIELDS,
            in_specs=[pl.BlockSpec(memory_space=pl.ANY)] * 7,
            out_specs=[pl.BlockSpec(memory_space=pltpu.VMEM)] * FIELDS,
            scratch_shapes=[
                *[pltpu.VMEM((CELLS + 8, LANES), f32)] * FIELDS,
                pltpu.VMEM((CELLS, LANES), f32),
                pltpu.VMEM((2 * ROWS, LANES), jnp.int32),
                pltpu.VMEM((ROWS, LANES), jnp.int32),
                pltpu.VMEM((FIELDS, CELLS, LANES), f32),
                pltpu.VMEM((CELLS, LANES), f32),
                pltpu.VMEM((CELLS, LANES), f32),
                pltpu.VMEM((CELLS, LANES), f32),
                pltpu.VMEM((2, MASK_ROW + 8, LANES), f32),
                pltpu.VMEM((2, MASK_ROW + 8, LANES), f32),
                pltpu.VMEM((2, 2 * ROWS, LANES), f32),
                pltpu.VMEM((2, 2 * ROWS, LANES), f32),
                pltpu.VMEM((2, ROWS, LANES), f32),
                pltpu.SemaphoreType.DMA((7,)),
                pltpu.SemaphoreType.DMA((4,)),
                pltpu.SemaphoreType.DMA((4,)),
            ],
            compiler_params=pltpu.CompilerParams(
                collective_id=0, has_side_effects=True, vmem_limit_bytes=16 * 1024 * 1024
            ),
        )(*[pltpu.with_memory_space_constraint(x, pltpu.HBM) for x in (*flat, bottom)])
        return tuple(x.reshape(LEVELS, ROWS, LANES) for x in outs)

    tile = P(None, "lat", "lon")
    return jax.shard_map(
        step,
        mesh=mesh,
        in_specs=(tile,) * 6 + (P("lat", "lon"),),
        out_specs=(tile,) * 4,
        check_vma=False,
    )
```

profile of v0, /device:TPU:1, one launch (start us, length us, event | category | flops | bytes accessed | tf_op | source)
XLA Modules:
  0.0 26.3 jit_solution(7518024091468837055)
XLA Ops:
  0.6 22.5 %shard_map.102 = (f32[1024,128]{1,0:T(8,128)S(1)}, f32[1024,128]{1,0:T(8,128)S(1)}, f32[1024,128]{1,0:T(8,128)S(1)}, f32[1024,128]{1,0:T(8,128)S(1)}) custom-call(f32[1024,128]{1,0:T(8,128)} %bitcast.14, f32[1024,128]{1,0:T(8,128)} %bitcast.15, f32[1024,128]{1,0:T(8,128)} %bitcast.16, f32[1024,128]{1,0:T(8,128)} %bitcast.17, f32[1024,128]{1,0:T(8,128)} %bitcast.18, ...), custom_call_target="tpu_custom_call" | custom-call | tf_op jit(solution)/shard_map/pallas_call | solution.py:500
  23.1 0.8 %copy.15 = f32[32,32,128]{2,1,0:T(8,128)} copy(f32[32,32,128]{2,1,0:T(8,128)S(1)} %bitcast.13) | data formatting | bytes 1048576
  23.9 0.8 %copy.16 = f32[32,32,128]{2,1,0:T(8,128)} copy(f32[32,32,128]{2,1,0:T(8,128)S(1)} %bitcast.12) | data formatting | bytes 1048576
  24.7 0.8 %copy.17 = f32[32,32,128]{2,1,0:T(8,128)} copy(f32[32,32,128]{2,1,0:T(8,128)S(1)} %bitcast.11) | data formatting | bytes 1048576
  25.5 0.8 %copy.18 = f32[32,32,128]{2,1,0:T(8,128)} copy(f32[32,32,128]{2,1,0:T(8,128)S(1)} %bitcast.10) | data formatting | bytes 1048576
where the time goes:
time: 26.5 us; the launch traced here: 26.3 us
  Pallas kernels  22.5 us (85%)
  local copies, waits for them, and re-layouts  3.17 us (12%)
  between operations  0.64 us (2%)
    pallas_call x1, Pallas kernels, step(): pl.pallas_call(functools.partial(kernel, lat_count, lon_count), out_shape...  22.5 us
    unnamed x4, local copies, waits for them, and re-layouts  3.17 us

commit v1 on v0

--- a/solution.py
+++ b/solution.py
@@ -30,6 +30,7 @@
 CELLS = LEVELS * ROWS
 FIELDS = 4
 MASK_ROW = FIELDS * LEVELS
+EDGE = 16
 PRESSURE_SCALE = 0.5 / LEVELS * (0.5 * GRADIENT / VISCOUS)
 FACE = 0.25 * ADVECT / DIFFUSE
 
@@ -72,6 +73,7 @@
     salt_out,
     zonal_out,
     merid_out,
+    col_out,
     warm,
     salt,
     zonal,
@@ -79,7 +81,6 @@
     mixing,
     top_open,
     bottom,
-    stars,
     link,
     inv_tracer,
     inv_momentum,
@@ -87,7 +88,11 @@
     row_recv,
     col_send,
     col_recv,
-    col_fix,
+    edge_inv,
+    edge_down,
+    edge_up,
+    edge_value,
+    square,
     load_sem,
     send_sem,
     recv_sem,
@@ -102,6 +107,8 @@
     north_lat = jnp.minimum(lat + 1, lat_count - 1)
     north_lon = jnp.where(is_north, lon_count - 1 - lon, lon)
     north = {"lat": north_lat, "lon": north_lon}
+    fields = (warm, salt, zonal, merid)
+    outs = (warm_out, salt_out, zonal_out, merid_out)
 
     loads = [
         pltpu.make_async_copy(src, dst, load_sem.at[n])
@@ -128,9 +135,9 @@
     def _():
         pl.semaphore_signal(barrier, inc=1, device_id=south, device_id_type=MESH)
 
-    fields = (warm, salt, zonal, merid)
     lane = iota(1)
     row = iota(0)
+    nothing = jnp.zeros((ROWS, LANES), jnp.float32)
     for field in fields:
         field[pl.ds(CELLS, 8)] = jnp.zeros((8, LANES), jnp.float32)
 
@@ -143,18 +150,46 @@
         math.pi / 180.0 * (-80.0 + 170.0 * (row_global + 0.5) / (ROWS * lat_count))
     )
 
-    for load in loads:
-        load.wait()
-
+    def at_level(k):
+        return pl.ds(pl.multiple_of(k * ROWS, ROWS), ROWS)
+
+    def pack(source, n, sums):
+        def one(k, sums):
+            easts, wests = sums
+            at = n * LEVELS + k
+            turned = pltpu.roll(source(k), at + 1, axis=1)
+            easts = jnp.where(lane == at, turned, easts)
+            wests = jnp.where(lane == lax.rem(at + 1, LANES), turned, wests)
+            return easts, wests
+
+        return lax.fori_loop(0, LEVELS, one, sums, unroll=8)
+
+    loads[0].wait()
+    loads[1].wait()
     deep = bottom[...].astype(jnp.float32)
     open0 = top_open[pl.ds(0, ROWS)].astype(jnp.float32)
     open1 = top_open[pl.ds(ROWS, ROWS)].astype(jnp.float32)
+    mask_planes = (deep, open0, open1)
     for side, edge in ((0, 0), (1, ROWS - 1)):
-        for n, field in enumerate(fields):
-            row_send[side, pl.ds(n * LEVELS, LEVELS)] = field[pl.ds(edge, LEVELS, stride=ROWS)]
-        for n, plane in enumerate((deep, open0, open1)):
+        for n, plane in enumerate(mask_planes):
             row_send[side, pl.ds(MASK_ROW + n, 1)] = plane[edge : edge + 1]
         row_send[side, pl.ds(MASK_ROW + 3, 5)] = jnp.zeros((5, LANES), jnp.float32)
+    east_masks = nothing
+    west_masks = nothing
+    for n, plane in enumerate(mask_planes):
+        turned = pltpu.roll(plane, n + 1, axis=1)
+        east_masks = jnp.where(lane == n, turned, east_masks)
+        west_masks = jnp.where(lane == n + 1, turned, west_masks)
+    col_send[1, pl.ds(ROWS, ROWS)] = east_masks
+    col_send[0, pl.ds(ROWS, ROWS)] = west_masks
+    packed = (nothing, nothing)
+    for n, field in enumerate(fields):
+        loads[2 + n].wait()
+        for side, edge in ((0, 0), (1, ROWS - 1)):
+            row_send[side, pl.ds(n * LEVELS, LEVELS)] = field[pl.ds(edge, LEVELS, stride=ROWS)]
+        packed = pack(lambda k, field=field: field[at_level(k)], n, packed)
+    col_send[1, pl.ds(0, ROWS)] = packed[0]
+    col_send[0, pl.ds(0, ROWS)] = packed[1]
 
     @pl.when(is_north)
     def _():
@@ -176,7 +211,6 @@
         device_id=north,
         device_id_type=MESH,
     )
-    to_north.start()
     to_south = pltpu.make_async_remote_copy(
         src_ref=row_send.at[0],
         dst_ref=row_recv.at[1],
@@ -185,32 +219,6 @@
         device_id=south,
         device_id_type=MESH,
     )
-
-    @pl.when(lat > 0)
-    def _():
-        to_south.start()
-
-    def pack(k, sums):
-        easts, wests = sums
-        for n, field in enumerate(fields):
-            at = n * LEVELS + k
-            turned = pltpu.roll(field[pl.ds(pl.multiple_of(k * ROWS, ROWS), ROWS)], at + 1, axis=1)
-            easts = jnp.where(lane == at, turned, easts)
-            wests = jnp.where(lane == lax.rem(at + 1, LANES), turned, wests)
-        return easts, wests
-
-    nothing = jnp.zeros((ROWS, LANES), jnp.float32)
-    easts, wests = lax.fori_loop(0, LEVELS, pack, (nothing, nothing), unroll=4)
-    col_send[1, pl.ds(0, ROWS)] = easts
-    col_send[0, pl.ds(0, ROWS)] = wests
-    east_masks = nothing
-    west_masks = nothing
-    for n, plane in enumerate((deep, open0, open1)):
-        turned = pltpu.roll(plane, n + 1, axis=1)
-        east_masks = jnp.where(lane == n, turned, east_masks)
-        west_masks = jnp.where(lane == n + 1, turned, west_masks)
-    col_send[1, pl.ds(ROWS, ROWS)] = east_masks
-    col_send[0, pl.ds(ROWS, ROWS)] = west_masks
     to_east = pltpu.make_async_remote_copy(
         src_ref=col_send.at[1],
         dst_ref=col_recv.at[0],
@@ -227,9 +235,16 @@
         device_id=west,
         device_id_type=MESH,
     )
+    to_north.start()
+
+    @pl.when(lat > 0)
+    def _():
+        to_south.start()
+
     to_east.start()
     to_west.start()
 
+    loads[6].wait()
     depth_here = bottom[...]
     not_east = lane < LANES - 1
     not_north = row < ROWS - 1
@@ -239,6 +254,7 @@
     depth_north = jnp.where(
         not_north, jnp.minimum(depth_here, pltpu.roll(depth_here, ROWS - 1, axis=0)), 0
     )
+    link[pl.ds(0, ROWS)] = nothing
 
     def level(k, masks, carried):
         above, g_above, pressure_sum = carried
@@ -272,8 +288,8 @@
             f_n = ahead_n * q_n + behind_n * q
             return jnp.where(wet, q - DIFFUSE * spread(f_e, f_n), 0.0)
 
-        stars[0, here] = tracer(t, t_e, t_n)
-        stars[1, here] = tracer(s, s_e, s_n)
+        warm_out[here] = tracer(t, t_e, t_n)
+        salt_out[here] = tracer(s, s_e, s_n)
 
         du_e = jnp.where(wet_east, u_e - u, 0.0)
         dp_e = jnp.where(wet_east, p_e - pressure, 0.0)
@@ -281,21 +297,21 @@
         lap_u = ((du_e - dp_e) - pltpu.roll(du_e + dp_e, 1, axis=1)) + (
             du_n - pltpu.roll(du_n, 1, axis=0)
         )
-        stars[2, here] = jnp.where(wet, u + VISCOUS * lap_u + coriolis * v, 0.0)
+        zonal_out[here] = jnp.where(wet, u + VISCOUS * lap_u + coriolis * v, 0.0)
         dv_n = jnp.where(wet_north, v_n - v, 0.0)
         dp_n = jnp.where(wet_north, p_n - pressure, 0.0)
         dv_e = jnp.where(wet_east, v_e - v, 0.0)
         lap_v = ((dv_n - dp_n) - pltpu.roll(dv_n + dp_n, 1, axis=0)) + (
             dv_e - pltpu.roll(dv_e, 1, axis=1)
         )
-        stars[3, here] = jnp.where(wet, v + VISCOUS * lap_v - coriolis * u, 0.0)
+        merid_out[here] = jnp.where(wet, v + VISCOUS * lap_v - coriolis * u, 0.0)
 
         below = jnp.where(wet_below, mixing[here], 0.0)
         diagonal = (1.0 + below) + above * (1.0 - g_above)
         inv = inverse(diagonal)
         dragged = jnp.logical_and(depth_here == k + 1, wet)
         inv_m = inverse(diagonal + jnp.where(dragged, BOTTOM_DRAG, 0.0))
-        link[here] = below
+        link[pl.ds(start + ROWS, ROWS)] = below
         inv_tracer[here] = inv
         inv_momentum[here] = inv_m
         return below, below * inv, pressure_sum
@@ -319,6 +335,89 @@
         return level(k, masks, carried)
 
     lax.fori_loop(2, LEVELS, deeper, carried)
+
+    def forward(k, values):
+        here = at_level(k)
+        above = link[here]
+        invs = (inv_tracer[here], inv_momentum[here])
+        new = []
+        for n in range(FIELDS):
+            value = (outs[n][here] + above * values[n]) * invs[n // 2]
+            outs[n][here] = value
+            new.append(value)
+        return tuple(new)
+
+    values = lax.fori_loop(0, LEVELS, forward, (nothing,) * 4, unroll=2)
+
+    def backward(step, values):
+        k = LEVELS - 2 - step
+        here = at_level(k)
+        ratio = link[at_level(k + 1)] * inv_tracer[here]
+        new = []
+        for n in range(FIELDS):
+            value = outs[n][here] + ratio * values[n]
+            outs[n][here] = value
+            new.append(value)
+        return tuple(new)
+
+    lax.fori_loop(0, LEVELS - 1, backward, values, unroll=2)
+
+    for side, edge in ((0, 0), (1, ROWS - 1)):
+        there = pl.ds(edge, LEVELS, stride=ROWS)
+        above = link[there]
+        below = link[pl.ds(ROWS + edge, LEVELS, stride=ROWS)]
+        inv_t = inv_tracer[there]
+        inv_m = inv_momentum[there]
+        up = below * inv_t
+        for n in range(FIELDS):
+            to = pl.ds(side * FIELDS + n, LEVELS, stride=EDGE)
+            edge_inv[to] = inv_m if n > 1 else inv_t
+            edge_down[to] = above * (inv_m if n > 1 else inv_t)
+            edge_up[to] = up
+    packed = (nothing, nothing)
+    packed = pack(lambda k: link[at_level(k)], 0, packed)
+    packed = pack(lambda k: inv_tracer[at_level(k)], 1, packed)
+    packed = pack(lambda k: inv_momentum[at_level(k)], 2, packed)
+    packed = pack(lambda k: link[at_level(k + 1)], 3, packed)
+
+    def side_by_side(wests, easts):
+        square[pl.ds(0, ROWS)] = wests
+        square[pl.ds(ROWS, ROWS)] = easts
+        square[pl.ds(2 * ROWS, ROWS)] = nothing
+        square[pl.ds(3 * ROWS, ROWS)] = nothing
+        return square[...].T
+
+    coefs = side_by_side(pltpu.roll(packed[1], LANES - 1, axis=1), packed[0])
+    above, inv_t, inv_m, below = (coefs[n * LEVELS : (n + 1) * LEVELS] for n in range(4))
+    for n in range(FIELDS):
+        to = pl.ds(2 * FIELDS + n, LEVELS, stride=EDGE)
+        edge_inv[to] = inv_m if n > 1 else inv_t
+        edge_down[to] = above * (inv_m if n > 1 else inv_t)
+        edge_up[to] = below * inv_t
+        spare = pl.ds(3 * FIELDS + n, LEVELS, stride=EDGE)
+        edge_down[spare] = nothing
+        edge_up[spare] = nothing
+        edge_value[spare] = nothing
+
+    def wet_levels(level_index, depth, first, second):
+        return jnp.where(
+            level_index == 0,
+            first,
+            jnp.where(
+                level_index == 1,
+                second,
+                jnp.where(level_index.astype(jnp.float32) < depth, 1.0, 0.0),
+            ),
+        )
+
+    def summed(half, axis, index):
+        total = half
+        for step in (1, 2, 4, 8, 16):
+            total = total + jnp.where(index >= step, pltpu.roll(total, step, axis=axis), 0.0)
+        return 2.0 * total - half
+
+    def edge_faces(q, q_o, a, face):
+        return jnp.where(face, (a - 1.0) * q_o + (a + 1.0) * q, 0.0)
 
     pltpu.make_async_remote_copy(
         src_ref=row_send.at[1],
@@ -340,47 +439,29 @@
             device_id_type=MESH,
         ).wait_recv()
 
-    def wet_levels(level_index, depth, first, second):
-        return jnp.where(
-            level_index == 0,
-            first,
-            jnp.where(
-                level_index == 1,
-                second,
-                jnp.where(level_index.astype(jnp.float32) < depth, 1.0, 0.0),
-            ),
-        )
-
-    def summed(half, axis, index):
-        total = half
-        for step in (1, 2, 4, 8, 16):
-            total = total + jnp.where(index >= step, pltpu.roll(total, step, axis=axis), 0.0)
-        return 2.0 * total - half
-
-    def edge_faces(q, q_o, a, face):
-        return jnp.where(face, (a - 1.0) * q_o + (a + 1.0) * q, 0.0)
-
+    row_float = row.astype(jnp.float32)
     for side, edge in ((0, 0), (1, ROWS - 1)):
         there = pl.ds(edge, LEVELS, stride=ROWS)
         own = [field[there] for field in fields]
         other = [row_recv[side, pl.ds(n * LEVELS, LEVELS)] for n in range(FIELDS)]
-        own_wet = wet_levels(row, deep[edge : edge + 1], open0[edge : edge + 1], open1[edge : edge + 1])
+        own_wet = wet_levels(row, *(plane[edge : edge + 1] for plane in mask_planes))
         other_wet = wet_levels(
             row, *(row_recv[side, pl.ds(MASK_ROW + n, 1)] for n in range(3))
         )
-        own_p = summed(half_density(own[0], own[1], own_wet > 0.5, row.astype(jnp.float32)), 0, row)
-        other_p = summed(
-            half_density(other[0], other[1], other_wet > 0.5, row.astype(jnp.float32)), 0, row
-        )
+        own_p = summed(half_density(own[0], own[1], own_wet > 0.5, row_float), 0, row)
+        other_p = summed(half_density(other[0], other[1], other_wet > 0.5, row_float), 0, row)
         face = own_wet * other_wet > 0.5
         sign = 1.0 if side else -1.0
         a = (sign * FACE) * (own[3] + other[3])
-        for n in (0, 1):
-            stars[n, there] += -DIFFUSE * edge_faces(own[n], other[n], a, face)
-        stars[2, there] += jnp.where(face, VISCOUS * (other[2] - own[2]), 0.0)
-        stars[3, there] += jnp.where(
-            face, VISCOUS * ((other[3] - own[3]) - sign * (other_p - own_p)), 0.0
-        )
+        fixes = (
+            -DIFFUSE * edge_faces(own[0], other[0], a, face),
+            -DIFFUSE * edge_faces(own[1], other[1], a, face),
+            jnp.where(face, VISCOUS * (other[2] - own[2]), 0.0),
+            jnp.where(face, VISCOUS * ((other[3] - own[3]) - sign * (other_p - own_p)), 0.0),
+        )
+        for n, fix in enumerate(fixes):
+            to = pl.ds(side * FIELDS + n, LEVELS, stride=EDGE)
+            edge_value[to] = fix * edge_inv[to]
 
     for side, sem in ((0, 2), (1, 3)):
         pltpu.make_async_remote_copy(
@@ -439,47 +520,44 @@
         )
         currents = jnp.where(face, VISCOUS * jump, 0.0)
         fixes.append(jnp.where(lane < 2 * LEVELS, tracers, currents))
-    west_fix = pltpu.roll(fixes[0], 1, axis=1)
-    east_fix = fixes[1]
+    turned = side_by_side(*fixes)
+    for n in range(FIELDS):
+        to = pl.ds(2 * FIELDS + n, LEVELS, stride=EDGE)
+        edge_value[to] = turned[n * LEVELS : (n + 1) * LEVELS] * edge_inv[to]
+
+    def edge_level(k):
+        return pl.ds(pl.multiple_of(k * EDGE, EDGE), EDGE)
+
+    def edge_forward(k, value):
+        here = edge_level(k)
+        value = edge_value[here] + edge_down[here] * value
+        edge_value[here] = value
+        return value
+
+    value = lax.fori_loop(
+        0, LEVELS, edge_forward, jnp.zeros((EDGE, LANES), jnp.float32), unroll=8
+    )
+
+    def edge_backward(step, value):
+        here = edge_level(LEVELS - 2 - step)
+        value = edge_value[here] + edge_up[here] * value
+        edge_value[here] = value
+        return value
+
+    lax.fori_loop(0, LEVELS - 1, edge_backward, value, unroll=8)
+
+    for side, edge in ((0, 0), (1, ROWS - 1)):
+        there = pl.ds(edge, LEVELS, stride=ROWS)
+        for n in range(FIELDS):
+            outs[n][there] += edge_value[pl.ds(side * FIELDS + n, LEVELS, stride=EDGE)]
+    for n in range(FIELDS):
+        square[pl.ds(n * LEVELS, LEVELS)] = edge_value[pl.ds(2 * FIELDS + n, LEVELS, stride=EDGE)]
+    turned = square[...].T
+    west_fix = pltpu.roll(turned[:ROWS], 1, axis=1)
+    east_fix = turned[ROWS : 2 * ROWS]
     even_lane = lax.rem(lane, 2) == 0
-    col_fix[0] = jnp.where(even_lane, east_fix, west_fix)
-    col_fix[1] = jnp.where(even_lane, west_fix, east_fix)
-
-    edge_lane = jnp.logical_or(lane == 0, lane == LANES - 1)
-
-    def forward(k, carried):
-        above, *values = carried
-        here = pl.ds(pl.multiple_of(k * ROWS, ROWS), ROWS)
-        fix = col_fix[lax.rem(k, 2)]
-        invs = (inv_tracer[here], inv_momentum[here])
-        new = []
-        for n in range(FIELDS):
-            turned = pltpu.roll(fix, LANES - 1 - n * LEVELS - k, axis=1)
-            star = stars[n, here] + jnp.where(edge_lane, turned, 0.0)
-            value = (star + above * values[n]) * invs[n // 2]
-            stars[n, here] = value
-            new.append(value)
-        return (link[here], *new)
-
-    _, *values = lax.fori_loop(0, LEVELS, forward, (nothing,) * 5)
-
-    outs = (warm_out, salt_out, zonal_out, merid_out)
-    last = pl.ds(CELLS - ROWS, ROWS)
-    for n in range(FIELDS):
-        outs[n][last] = values[n]
-
-    def backward(step, values):
-        k = LEVELS - 2 - step
-        here = pl.ds(pl.multiple_of(k * ROWS, ROWS), ROWS)
-        ratio = link[here] * inv_tracer[here]
-        new = []
-        for n in range(FIELDS):
-            value = stars[n, here] + ratio * values[n]
-            outs[n][here] = value
-            new.append(value)
-        return tuple(new)
-
-    lax.fori_loop(0, LEVELS - 1, backward, tuple(values))
+    col_out[pl.ds(0, ROWS)] = jnp.where(even_lane, east_fix, west_fix)
+    col_out[pl.ds(ROWS, ROWS)] = jnp.where(even_lane, west_fix, east_fix)
 
     to_north.wait_send()
     to_east.wait_send()
@@ -490,6 +568,39 @@
         to_south.wait_send()
 
 
+def finish(warm, salt, zonal, merid, col_fix, warm_hbm, salt_hbm, zonal_hbm, merid_hbm, done, sem):
+    lane = iota(1)
+    edge_lane = jnp.logical_or(lane == 0, lane == LANES - 1)
+    sources = (warm, salt, zonal, merid)
+    targets = (warm_hbm, salt_hbm, zonal_hbm, merid_hbm)
+    stores = []
+    for n in range(FIELDS):
+
+        def add(pair, _, n=n):
+            for odd in range(2):
+                k = 2 * pair + odd
+                here = pl.ds(pl.multiple_of(k * ROWS, ROWS), ROWS)
+                fix = col_fix[pl.ds(odd * ROWS, ROWS)]
+                turned = pltpu.roll(fix, LANES - 1 - n * LEVELS - k, axis=1)
+                done[n, here] = sources[n][here] + jnp.where(edge_lane, turned, 0.0)
+            return 0
+
+        lax.fori_loop(0, LEVELS // 2, add, 0, unroll=4)
+        store = pltpu.make_async_copy(done.at[n], targets[n], sem.at[n])
+        store.start()
+        stores.append(store)
+    for store in stores:
+        store.wait()
+
+
+def result(space, rows):
+    return space((rows, LANES), jnp.float32)
+
+
+def keep_in(x, space):
+    return pltpu.with_memory_space_constraint(x, space)
+
+
 def solution(mesh):
     lat_count = mesh.shape["lat"]
     lon_count = mesh.shape["lon"]
@@ -497,25 +608,28 @@
     def step(warm, salt, zonal, merid, mixing, open_water, bottom):
         flat = [x.reshape(CELLS, LANES) for x in (warm, salt, zonal, merid, mixing, open_water)]
         f32 = jnp.float32
-        outs = pl.pallas_call(
+        solved = pl.pallas_call(
             functools.partial(kernel, lat_count, lon_count),
-            out_shape=[pltpu.VMEM((CELLS, LANES), f32)] * FIELDS,
+            out_shape=[
+                *[result(pltpu.VMEM, CELLS)] * FIELDS,
+                result(pltpu.VMEM, 2 * ROWS),
+            ],
             in_specs=[pl.BlockSpec(memory_space=pl.ANY)] * 7,
-            out_specs=[pl.BlockSpec(memory_space=pltpu.VMEM)] * FIELDS,
+            out_specs=[pl.BlockSpec(memory_space=pltpu.VMEM)] * (FIELDS + 1),
             scratch_shapes=[
                 *[pltpu.VMEM((CELLS + 8, LANES), f32)] * FIELDS,
                 pltpu.VMEM((CELLS, LANES), f32),
                 pltpu.VMEM((2 * ROWS, LANES), jnp.int32),
                 pltpu.VMEM((ROWS, LANES), jnp.int32),
-                pltpu.VMEM((FIELDS, CELLS, LANES), f32),
-                pltpu.VMEM((CELLS, LANES), f32),
+                pltpu.VMEM((CELLS + ROWS, LANES), f32),
                 pltpu.VMEM((CELLS, LANES), f32),
                 pltpu.VMEM((CELLS, LANES), f32),
                 pltpu.VMEM((2, MASK_ROW + 8, LANES), f32),
                 pltpu.VMEM((2, MASK_ROW + 8, LANES), f32),
                 pltpu.VMEM((2, 2 * ROWS, LANES), f32),
                 pltpu.VMEM((2, 2 * ROWS, LANES), f32),
-                pltpu.VMEM((2, ROWS, LANES), f32),
+                *[pltpu.VMEM((LEVELS * EDGE, LANES), f32)] * 4,
+                pltpu.VMEM((LANES, LANES), f32),
                 pltpu.SemaphoreType.DMA((7,)),
                 pltpu.SemaphoreType.DMA((4,)),
                 pltpu.SemaphoreType.DMA((4,)),
@@ -523,7 +637,18 @@
             compiler_params=pltpu.CompilerParams(
                 collective_id=0, has_side_effects=True, vmem_limit_bytes=16 * 1024 * 1024
             ),
-        )(*[pltpu.with_memory_space_constraint(x, pltpu.HBM) for x in (*flat, bottom)])
+        )(*[keep_in(x, pltpu.HBM) for x in (*flat, bottom)])
+        outs = pl.pallas_call(
+            finish,
+            out_shape=[result(pltpu.HBM, CELLS)] * FIELDS,
+            in_specs=[pl.BlockSpec(memory_space=pltpu.VMEM)] * (FIELDS + 1),
+            out_specs=[pl.BlockSpec(memory_space=pltpu.HBM)] * FIELDS,
+            scratch_shapes=[
+                pltpu.VMEM((FIELDS, CELLS, LANES), f32),
+                pltpu.SemaphoreType.DMA((FIELDS,)),
+            ],
+            compiler_params=pltpu.CompilerParams(vmem_limit_bytes=8 * 1024 * 1024),
+        )(*[keep_in(x, pltpu.VMEM) for x in solved])
         return tuple(x.reshape(LEVELS, ROWS, LANES) for x in outs)
 
     tile = P(None, "lat", "lon")

time: 26.5 us -> 24.5 us (0.925)
  local copies, waits for them, and re-layouts: 3.17 us -> 0 us
  Pallas kernels: 22.5 us -> 23.7 us
    unnamed x4 -> x0, local copies, waits for them, and re-layouts: 3.17 us -> none
    pallas_call x0 -> x1, Pallas kernels: none -> 2.48 us  [step(): pl.pallas_call(finish, out_shape=[result(pltpu.HBM, CELLS)] * FIELDS, in_...]
    pallas_call x1, Pallas kernels: 22.5 us -> 21.2 us  [step(): pl.pallas_call(functools.partial(kernel, lat_count, lon_count), out_shape...]
where the time goes in v1:
time: 24.5 us; the launch traced here: 24.4 us
  Pallas kernels  23.7 us (97%)
  between operations  0.64 us (3%)
    pallas_call x1, Pallas kernels, step(): pl.pallas_call(functools.partial(kernel, lat_count, lon_count), out_shape...  21.2 us
    pallas_call x1, Pallas kernels, step(): pl.pallas_call(finish, out_shape=[result(pltpu.HBM, CELLS)] * FIELDS, in_...  2.48 us

profile of v1, /device:TPU:1, one launch (start us, length us, event | category | flops | bytes accessed | tf_op | source)
XLA Modules:
  0.0 24.4 jit_solution(13132513093202011271)
XLA Ops:
  0.6 21.2 %shard_map.102 = (f32[1024,128]{1,0:T(8,128)S(1)}, f32[1024,128]{1,0:T(8,128)S(1)}, f32[1024,128]{1,0:T(8,128)S(1)}, f32[1024,128]{1,0:T(8,128)S(1)}, f32[64,128]{1,0:T(8,128)S(1)}) custom-call(f32[1024,128]{1,0:T(8,128)} %bitcast.10, f32[1024,128]{1,0:T(8,128)} %bitcast.11, f32[1024,128]{1,0:T(8,128)} %bitcast.12, f32[1024,128]{1,0:T(8,128)} %bitcast.13, ...), custom_call_target="tpu_custom_call" | custom-call | tf_op jit(solution)/shard_map/pallas_call | solution.py:611
  21.9 2.5 %shard_map.103 = (f32[1024,128]{1,0:T(8,128)}, f32[1024,128]{1,0:T(8,128)}, f32[1024,128]{1,0:T(8,128)}, f32[1024,128]{1,0:T(8,128)}) custom-call(f32[1024,128]{1,0:T(8,128)S(1)} %get-tuple-element.13.warm, f32[1024,128]{1,0:T(8,128)S(1)} %get-tuple-element.14.salt, f32[1024,128]{1,0:T(8,128)S(1)} %get-tuple-element.15.zonal, ...), custom_call_target="tpu_custom_call" | custom-call | tf_op jit(solution)/shard_map/pallas_call | solution.py:641

commit v2 on v1

--- a/solution.py
+++ b/solution.py
@@ -31,6 +31,8 @@
 FIELDS = 4
 MASK_ROW = FIELDS * LEVELS
 EDGE = 16
+UNROLL = 3
+FOLD_TURNS = (1, 3, 5, 3, 0, 0, 0, 0)
 PRESSURE_SCALE = 0.5 / LEVELS * (0.5 * GRADIENT / VISCOUS)
 FACE = 0.25 * ADVECT / DIFFUSE
 
@@ -110,6 +112,31 @@
     fields = (warm, salt, zonal, merid)
     outs = (warm_out, salt_out, zonal_out, merid_out)
 
+    span = lon_count // 2
+    place = lax.rem(lon, span)
+    lat_odd = lax.rem(lat, 2) == 1
+    answers_west = place == 0
+    fold_late = jnp.logical_and(is_north, place >= span // 2)
+    answers_north = jnp.logical_and(lat_odd, jnp.logical_not(fold_late))
+    first_west = jnp.logical_not(answers_west)
+    first_north = jnp.logical_not(answers_north)
+
+    barrier = pltpu.get_barrier_semaphore()
+
+    def greet(target):
+        pl.semaphore_signal(barrier, inc=1, device_id=target, device_id_type=MESH)
+
+    pl.when(jnp.logical_not(fold_late))(lambda: greet(north))
+    pl.when(lat_odd)(lambda: greet(south))
+    pl.when(place < span - 1)(lambda: greet(east))
+    greet(west)
+    greetings = (
+        1
+        + jnp.where(first_west, 1, 0)
+        + jnp.where(first_north, 1, 0)
+        + jnp.where(is_south, 0, 1)
+    )
+
     loads = [
         pltpu.make_async_copy(src, dst, load_sem.at[n])
         for n, (src, dst) in enumerate(
@@ -127,14 +154,6 @@
     for load in loads:
         load.start()
 
-    barrier = pltpu.get_barrier_semaphore()
-    for target in (east, west, north):
-        pl.semaphore_signal(barrier, inc=1, device_id=target, device_id_type=MESH)
-
-    @pl.when(lat > 0)
-    def _():
-        pl.semaphore_signal(barrier, inc=1, device_id=south, device_id_type=MESH)
-
     lane = iota(1)
     row = iota(0)
     nothing = jnp.zeros((ROWS, LANES), jnp.float32)
@@ -151,18 +170,16 @@
     )
 
     def at_level(k):
-        return pl.ds(pl.multiple_of(k * ROWS, ROWS), ROWS)
+        return pl.ds(k * ROWS if isinstance(k, int) else pl.multiple_of(k * ROWS, ROWS), ROWS)
 
     def pack(source, n, sums):
-        def one(k, sums):
-            easts, wests = sums
+        easts, wests = sums
+        for k in range(LEVELS):
             at = n * LEVELS + k
-            turned = pltpu.roll(source(k), at + 1, axis=1)
+            turned = pltpu.roll(source(k), (at + 1) % LANES, axis=1)
             easts = jnp.where(lane == at, turned, easts)
-            wests = jnp.where(lane == lax.rem(at + 1, LANES), turned, wests)
-            return easts, wests
-
-        return lax.fori_loop(0, LEVELS, one, sums, unroll=8)
+            wests = jnp.where(lane == (at + 1) % LANES, turned, wests)
+        return easts, wests
 
     loads[0].wait()
     loads[1].wait()
@@ -201,8 +218,6 @@
                 turned = -turned
             row_send[1, there] = turned
 
-    pl.semaphore_wait(barrier, jnp.where(is_south, 3, 4))
-
     to_north = pltpu.make_async_remote_copy(
         src_ref=row_send.at[1],
         dst_ref=row_recv.at[jnp.where(is_north, 1, 0)],
@@ -235,14 +250,21 @@
         device_id=west,
         device_id_type=MESH,
     )
-    to_north.start()
-
-    @pl.when(lat > 0)
-    def _():
-        to_south.start()
-
+    pl.semaphore_wait(barrier, greetings)
+    north_turn = 0
+    for n, turn in enumerate(FOLD_TURNS):
+        north_turn = jnp.where(jnp.logical_and(fold_late, place == span - 1 - n), turn, north_turn)
     to_east.start()
-    to_west.start()
+    pl.when(first_west)(to_west.start)
+    pl.when(jnp.logical_and(first_north, north_turn == 0))(to_north.start)
+    pl.when(lat > 0)(to_south.start)
+
+    def side_by_side(wests, easts):
+        square[pl.ds(0, ROWS)] = wests
+        square[pl.ds(ROWS, ROWS)] = easts
+        square[pl.ds(2 * ROWS, ROWS)] = nothing
+        square[pl.ds(3 * ROWS, ROWS)] = nothing
+        return square[...].T
 
     loads[6].wait()
     depth_here = bottom[...]
@@ -334,7 +356,13 @@
         masks = (depth_here > k, depth_east > k, depth_north > k, depth_here > k + 1)
         return level(k, masks, carried)
 
-    lax.fori_loop(2, LEVELS, deeper, carried)
+    def group(step, carried):
+        pl.when(jnp.logical_and(first_north, north_turn == step + 1))(to_north.start)
+        for n in range(UNROLL):
+            carried = deeper(2 + UNROLL * step + n, carried)
+        return carried
+
+    lax.fori_loop(0, (LEVELS - 2) // UNROLL, group, carried)
 
     def forward(k, values):
         here = at_level(k)
@@ -380,13 +408,6 @@
     packed = pack(lambda k: inv_momentum[at_level(k)], 2, packed)
     packed = pack(lambda k: link[at_level(k + 1)], 3, packed)
 
-    def side_by_side(wests, easts):
-        square[pl.ds(0, ROWS)] = wests
-        square[pl.ds(ROWS, ROWS)] = easts
-        square[pl.ds(2 * ROWS, ROWS)] = nothing
-        square[pl.ds(3 * ROWS, ROWS)] = nothing
-        return square[...].T
-
     coefs = side_by_side(pltpu.roll(packed[1], LANES - 1, axis=1), packed[0])
     above, inv_t, inv_m, below = (coefs[n * LEVELS : (n + 1) * LEVELS] for n in range(4))
     for n in range(FIELDS):
@@ -419,36 +440,72 @@
     def edge_faces(q, q_o, a, face):
         return jnp.where(face, (a - 1.0) * q_o + (a + 1.0) * q, 0.0)
 
-    pltpu.make_async_remote_copy(
-        src_ref=row_send.at[1],
-        dst_ref=row_recv.at[1],
-        send_sem=send_sem.at[1],
-        recv_sem=recv_sem.at[1],
-        device_id=north,
-        device_id_type=MESH,
-    ).wait_recv()
-
-    @pl.when(lat > 0)
+    def arrival(source, target, slot, sem):
+        return pltpu.make_async_remote_copy(
+            src_ref=source.at[slot],
+            dst_ref=target.at[slot],
+            send_sem=send_sem.at[sem],
+            recv_sem=recv_sem.at[sem],
+            device_id=east,
+            device_id_type=MESH,
+        )
+
+    from_south = arrival(row_send, row_recv, 0, 0)
+    from_north = arrival(row_send, row_recv, 1, 1)
+    from_west = arrival(col_send, col_recv, 0, 2)
+    from_east = arrival(col_send, col_recv, 1, 3)
+
+    row_float = row.astype(jnp.float32)
+    row_edges = []
+    for side, edge in ((0, 0), (1, ROWS - 1)):
+        own = [field[pl.ds(edge, LEVELS, stride=ROWS)] for field in fields]
+        wet = wet_levels(row, *(plane[edge : edge + 1] for plane in mask_planes))
+        pressure = summed(half_density(own[0], own[1], wet > 0.5, row_float), 0, row)
+        row_edges.append((own, wet, pressure))
+
+    level_lane = lax.rem(lane, LEVELS)
+    level_lane_float = level_lane.astype(jnp.float32)
+    first_group = lane < LEVELS
+
+    def spread_mask(mask):
+        return wet_levels(
+            level_lane,
+            *(jnp.broadcast_to(mask[:, n : n + 1], (ROWS, LANES)) for n in range(3)),
+        )
+
+    def pressure_of(packed, wet):
+        half = half_density(
+            packed,
+            pltpu.roll(packed, LANES - LEVELS, axis=1),
+            jnp.logical_and(wet > 0.5, first_group),
+            level_lane_float,
+        )
+        return summed(half, 1, lane)
+
+    col_edges = []
+    for side in (0, 1):
+        own = col_send[side, pl.ds(0, ROWS)]
+        mask = col_send[side, pl.ds(ROWS, ROWS)]
+        if side == 0:
+            own = pltpu.roll(own, LANES - 1, axis=1)
+            mask = pltpu.roll(mask, LANES - 1, axis=1)
+        wet = spread_mask(mask)
+        col_edges.append((own, wet, pressure_of(own, wet)))
+
+    @pl.when(answers_north)
     def _():
-        pltpu.make_async_remote_copy(
-            src_ref=row_send.at[0],
-            dst_ref=row_recv.at[0],
-            send_sem=send_sem.at[0],
-            recv_sem=recv_sem.at[0],
-            device_id=south,
-            device_id_type=MESH,
-        ).wait_recv()
-
-    row_float = row.astype(jnp.float32)
-    for side, edge in ((0, 0), (1, ROWS - 1)):
-        there = pl.ds(edge, LEVELS, stride=ROWS)
-        own = [field[there] for field in fields]
+        from_north.wait_recv()
+        to_north.start()
+
+    pl.when(first_north)(from_north.wait_recv)
+    pl.when(lat > 0)(from_south.wait_recv)
+
+    for side in (0, 1):
+        own, own_wet, own_p = row_edges[side]
         other = [row_recv[side, pl.ds(n * LEVELS, LEVELS)] for n in range(FIELDS)]
-        own_wet = wet_levels(row, *(plane[edge : edge + 1] for plane in mask_planes))
         other_wet = wet_levels(
             row, *(row_recv[side, pl.ds(MASK_ROW + n, 1)] for n in range(3))
         )
-        own_p = summed(half_density(own[0], own[1], own_wet > 0.5, row_float), 0, row)
         other_p = summed(half_density(other[0], other[1], other_wet > 0.5, row_float), 0, row)
         face = own_wet * other_wet > 0.5
         sign = 1.0 if side else -1.0
@@ -463,50 +520,25 @@
             to = pl.ds(side * FIELDS + n, LEVELS, stride=EDGE)
             edge_value[to] = fix * edge_inv[to]
 
-    for side, sem in ((0, 2), (1, 3)):
-        pltpu.make_async_remote_copy(
-            src_ref=col_send.at[side],
-            dst_ref=col_recv.at[side],
-            send_sem=send_sem.at[sem],
-            recv_sem=recv_sem.at[sem],
-            device_id=east,
-            device_id_type=MESH,
-        ).wait_recv()
-    level_lane = lax.rem(lane, LEVELS)
-    level_lane_float = level_lane.astype(jnp.float32)
-    first_group = lane < LEVELS
+    from_east.wait_recv()
+
+    @pl.when(answers_west)
+    def _():
+        from_west.wait_recv()
+        to_west.start()
+
+    pl.when(first_west)(from_west.wait_recv)
+
     fixes = []
     for side in (0, 1):
-        own = col_send[side, pl.ds(0, ROWS)]
+        own, own_wet, own_p = col_edges[side]
         other = col_recv[side, pl.ds(0, ROWS)]
-        own_mask = col_send[side, pl.ds(ROWS, ROWS)]
         other_mask = col_recv[side, pl.ds(ROWS, ROWS)]
-        if side == 0:
-            own = pltpu.roll(own, LANES - 1, axis=1)
-            own_mask = pltpu.roll(own_mask, LANES - 1, axis=1)
-        else:
+        if side == 1:
             other = pltpu.roll(other, LANES - 1, axis=1)
             other_mask = pltpu.roll(other_mask, LANES - 1, axis=1)
-
-        def spread_mask(mask):
-            return wet_levels(
-                level_lane,
-                *(jnp.broadcast_to(mask[:, n : n + 1], (ROWS, LANES)) for n in range(3)),
-            )
-
-        own_wet = spread_mask(own_mask)
         other_wet = spread_mask(other_mask)
-
-        def pressure_of(packed, wet):
-            half = half_density(
-                packed,
-                pltpu.roll(packed, LANES - LEVELS, axis=1),
-                jnp.logical_and(wet > 0.5, first_group),
-                level_lane_float,
-            )
-            return summed(half, 1, lane)
-
-        jump_p = pressure_of(other, other_wet) - pressure_of(own, own_wet)
+        jump_p = pressure_of(other, other_wet) - own_p
         face = own_wet * other_wet > 0.5
         sign = 1.0 if side else -1.0
         both = own + other
@@ -576,16 +608,11 @@
     stores = []
     for n in range(FIELDS):
 
-        def add(pair, _, n=n):
-            for odd in range(2):
-                k = 2 * pair + odd
-                here = pl.ds(pl.multiple_of(k * ROWS, ROWS), ROWS)
-                fix = col_fix[pl.ds(odd * ROWS, ROWS)]
-                turned = pltpu.roll(fix, LANES - 1 - n * LEVELS - k, axis=1)
-                done[n, here] = sources[n][here] + jnp.where(edge_lane, turned, 0.0)
-            return 0
-
-        lax.fori_loop(0, LEVELS // 2, add, 0, unroll=4)
+        for k in range(LEVELS):
+            here = pl.ds(k * ROWS, ROWS)
+            fix = col_fix[pl.ds(k % 2 * ROWS, ROWS)]
+            turned = pltpu.roll(fix, LANES - 1 - n * LEVELS - k, axis=1)
+            done[n, here] = sources[n][here] + jnp.where(edge_lane, turned, 0.0)
         store = pltpu.make_async_copy(done.at[n], targets[n], sem.at[n])
         store.start()
         stores.append(store)

time: 24.5 us -> 20.8 us (0.85)
  the two profiles are of different devices: /device:TPU:1 before, /device:TPU:61 now
where the time goes in v2:
time: 20.8 us; the launch traced here: 20.6 us
  Pallas kernels  20 us (96%)
  between operations  0.64 us (3%)
    pallas_call x1, Pallas kernels, step(): pl.pallas_call(functools.partial(kernel, lat_count, lon_count), out_shape...  18.4 us
    pallas_call x1, Pallas kernels, step(): pl.pallas_call(finish, out_shape=[result(pltpu.HBM, CELLS)] * FIELDS, in_...  1.55 us

profile of v2, /device:TPU:61, one launch (start us, length us, event | category | flops | bytes accessed | tf_op | source)
XLA Modules:
  0.0 20.6 jit_solution(16516803314354070793)
XLA Ops:
  0.6 18.4 %shard_map.102 = (f32[1024,128]{1,0:T(8,128)S(1)}, f32[1024,128]{1,0:T(8,128)S(1)}, f32[1024,128]{1,0:T(8,128)S(1)}, f32[1024,128]{1,0:T(8,128)S(1)}, f32[64,128]{1,0:T(8,128)S(1)}) custom-call(f32[1024,128]{1,0:T(8,128)} %bitcast.10, f32[1024,128]{1,0:T(8,128)} %bitcast.11, f32[1024,128]{1,0:T(8,128)} %bitcast.12, f32[1024,128]{1,0:T(8,128)} %bitcast.13, ...), custom_call_target="tpu_custom_call" | custom-call | tf_op jit(solution)/shard_map/pallas_call | solution.py:638
  19.1 1.5 %shard_map.103 = (f32[1024,128]{1,0:T(8,128)}, f32[1024,128]{1,0:T(8,128)}, f32[1024,128]{1,0:T(8,128)}, f32[1024,128]{1,0:T(8,128)}) custom-call(f32[1024,128]{1,0:T(8,128)S(1)} %get-tuple-element.13.warm, f32[1024,128]{1,0:T(8,128)S(1)} %get-tuple-element.14.salt, f32[1024,128]{1,0:T(8,128)S(1)} %get-tuple-element.15.zonal, ...), custom_call_target="tpu_custom_call" | custom-call | tf_op jit(solution)/shard_map/pallas_call | solution.py:668

commit v3 on v2

--- a/solution.py
+++ b/solution.py
@@ -32,7 +32,8 @@
 MASK_ROW = FIELDS * LEVELS
 EDGE = 16
 UNROLL = 3
-FOLD_TURNS = (1, 3, 5, 3, 0, 0, 0, 0)
+BLOCK = 4
+FOLD_TURNS = (0, 1, 3, 5, 0, 0, 0, 0)
 PRESSURE_SCALE = 0.5 / LEVELS * (0.5 * GRADIENT / VISCOUS)
 FACE = 0.25 * ADVECT / DIFFUSE
 
@@ -76,6 +77,7 @@
     zonal_out,
     merid_out,
     col_out,
+    edge_value,
     warm,
     salt,
     zonal,
@@ -93,11 +95,15 @@
     edge_inv,
     edge_down,
     edge_up,
-    edge_value,
-    square,
+    edge_down_block,
+    edge_up_block,
+    edge_half,
+    edge_weight,
     load_sem,
     send_sem,
     recv_sem,
+    go_west,
+    go_north,
 ):
     lat = lax.axis_index("lat")
     lon = lax.axis_index("lon")
@@ -114,8 +120,9 @@
 
     span = lon_count // 2
     place = lax.rem(lon, span)
+    is_last = place == span - 1
     lat_odd = lax.rem(lat, 2) == 1
-    answers_west = place == 0
+    answers_west = jnp.logical_or(place == 0, is_last)
     fold_late = jnp.logical_and(is_north, place >= span // 2)
     answers_north = jnp.logical_and(lat_odd, jnp.logical_not(fold_late))
     first_west = jnp.logical_not(answers_west)
@@ -128,7 +135,7 @@
 
     pl.when(jnp.logical_not(fold_late))(lambda: greet(north))
     pl.when(lat_odd)(lambda: greet(south))
-    pl.when(place < span - 1)(lambda: greet(east))
+    pl.when(place < span - 2)(lambda: greet(east))
     greet(west)
     greetings = (
         1
@@ -136,6 +143,18 @@
         + jnp.where(first_north, 1, 0)
         + jnp.where(is_south, 0, 1)
     )
+
+    meets_early = jnp.logical_and(is_last, lax.rem(lat, 4) != 0)
+
+    def meet():
+        pl.semaphore_wait(barrier, greetings)
+
+        def go(sem, target):
+            pl.semaphore_signal(sem, inc=1, device_id=target, device_id_type=MESH)
+
+        pl.when(place >= span - 2)(lambda: go(go_west, east))
+        pl.when(jnp.logical_and(jnp.logical_not(lat_odd), lat > 0))(lambda: go(go_north, south))
+        pl.when(fold_late)(lambda: go(go_north, north))
 
     loads = [
         pltpu.make_async_copy(src, dst, load_sem.at[n])
@@ -151,7 +170,7 @@
             )
         )
     ]
-    for load in loads:
+    for load in loads[:6]:
         load.start()
 
     lane = iota(1)
@@ -181,6 +200,7 @@
             wests = jnp.where(lane == (at + 1) % LANES, turned, wests)
         return easts, wests
 
+    pl.when(meets_early)(meet)
     loads[0].wait()
     loads[1].wait()
     deep = bottom[...].astype(jnp.float32)
@@ -197,16 +217,21 @@
         turned = pltpu.roll(plane, n + 1, axis=1)
         east_masks = jnp.where(lane == n, turned, east_masks)
         west_masks = jnp.where(lane == n + 1, turned, west_masks)
-    col_send[1, pl.ds(ROWS, ROWS)] = east_masks
-    col_send[0, pl.ds(ROWS, ROWS)] = west_masks
+    west_masks = pltpu.roll(west_masks, LANES - 1, axis=1)
+    turned = jnp.concatenate([east_masks, west_masks, west_masks, east_masks], axis=0).T[:8]
+    col_send[1, pl.ds(ROWS, 8)] = turned
+    col_send[0, pl.ds(ROWS, 8)] = turned
+    own_planes = pltpu.roll(turned, LANES - 2 * ROWS, axis=1)
     packed = (nothing, nothing)
     for n, field in enumerate(fields):
         loads[2 + n].wait()
+        if n == 1:
+            loads[6].start()
         for side, edge in ((0, 0), (1, ROWS - 1)):
             row_send[side, pl.ds(n * LEVELS, LEVELS)] = field[pl.ds(edge, LEVELS, stride=ROWS)]
         packed = pack(lambda k, field=field: field[at_level(k)], n, packed)
     col_send[1, pl.ds(0, ROWS)] = packed[0]
-    col_send[0, pl.ds(0, ROWS)] = packed[1]
+    col_send[0, pl.ds(0, ROWS)] = pltpu.roll(packed[1], LANES - 1, axis=1)
 
     @pl.when(is_north)
     def _():
@@ -250,7 +275,7 @@
         device_id=west,
         device_id_type=MESH,
     )
-    pl.semaphore_wait(barrier, greetings)
+    pl.when(jnp.logical_not(meets_early))(meet)
     north_turn = 0
     for n, turn in enumerate(FOLD_TURNS):
         north_turn = jnp.where(jnp.logical_and(fold_late, place == span - 1 - n), turn, north_turn)
@@ -259,12 +284,8 @@
     pl.when(jnp.logical_and(first_north, north_turn == 0))(to_north.start)
     pl.when(lat > 0)(to_south.start)
 
-    def side_by_side(wests, easts):
-        square[pl.ds(0, ROWS)] = wests
-        square[pl.ds(ROWS, ROWS)] = easts
-        square[pl.ds(2 * ROWS, ROWS)] = nothing
-        square[pl.ds(3 * ROWS, ROWS)] = nothing
-        return square[...].T
+    def levels_first(wests, easts):
+        return jnp.concatenate([wests, easts, nothing, nothing], axis=0).T
 
     loads[6].wait()
     depth_here = bottom[...]
@@ -408,7 +429,7 @@
     packed = pack(lambda k: inv_momentum[at_level(k)], 2, packed)
     packed = pack(lambda k: link[at_level(k + 1)], 3, packed)
 
-    coefs = side_by_side(pltpu.roll(packed[1], LANES - 1, axis=1), packed[0])
+    coefs = levels_first(pltpu.roll(packed[1], LANES - 1, axis=1), packed[0])
     above, inv_t, inv_m, below = (coefs[n * LEVELS : (n + 1) * LEVELS] for n in range(4))
     for n in range(FIELDS):
         to = pl.ds(2 * FIELDS + n, LEVELS, stride=EDGE)
@@ -419,6 +440,21 @@
         edge_down[spare] = nothing
         edge_up[spare] = nothing
         edge_value[spare] = nothing
+    edge_half[...] = jnp.zeros_like(edge_half)
+    edge_weight[...] = jnp.zeros_like(edge_weight)
+
+    def edge_level(k):
+        return pl.ds(k * EDGE, EDGE)
+
+    for start in range(0, LEVELS, BLOCK):
+        down = up = None
+        for n in range(BLOCK):
+            k = start + n
+            down = edge_down[edge_level(k)] if n == 0 else down * edge_down[edge_level(k)]
+            edge_down_block[edge_level(k)] = down
+            k = start + BLOCK - 1 - n
+            up = edge_up[edge_level(k)] if n == 0 else up * edge_up[edge_level(k)]
+            edge_up_block[edge_level(k)] = up
 
     def wet_levels(level_index, depth, first, second):
         return jnp.where(
@@ -431,15 +467,6 @@
             ),
         )
 
-    def summed(half, axis, index):
-        total = half
-        for step in (1, 2, 4, 8, 16):
-            total = total + jnp.where(index >= step, pltpu.roll(total, step, axis=axis), 0.0)
-        return 2.0 * total - half
-
-    def edge_faces(q, q_o, a, face):
-        return jnp.where(face, (a - 1.0) * q_o + (a + 1.0) * q, 0.0)
-
     def arrival(source, target, slot, sem):
         return pltpu.make_async_remote_copy(
             src_ref=source.at[slot],
@@ -456,135 +483,99 @@
     from_east = arrival(col_send, col_recv, 1, 3)
 
     row_float = row.astype(jnp.float32)
-    row_edges = []
-    for side, edge in ((0, 0), (1, ROWS - 1)):
-        own = [field[pl.ds(edge, LEVELS, stride=ROWS)] for field in fields]
-        wet = wet_levels(row, *(plane[edge : edge + 1] for plane in mask_planes))
-        pressure = summed(half_density(own[0], own[1], wet > 0.5, row_float), 0, row)
-        row_edges.append((own, wet, pressure))
-
-    level_lane = lax.rem(lane, LEVELS)
-    level_lane_float = level_lane.astype(jnp.float32)
-    first_group = lane < LEVELS
-
-    def spread_mask(mask):
-        return wet_levels(
-            level_lane,
-            *(jnp.broadcast_to(mask[:, n : n + 1], (ROWS, LANES)) for n in range(3)),
-        )
-
-    def pressure_of(packed, wet):
-        half = half_density(
-            packed,
-            pltpu.roll(packed, LANES - LEVELS, axis=1),
-            jnp.logical_and(wet > 0.5, first_group),
-            level_lane_float,
-        )
-        return summed(half, 1, lane)
-
-    col_edges = []
-    for side in (0, 1):
-        own = col_send[side, pl.ds(0, ROWS)]
-        mask = col_send[side, pl.ds(ROWS, ROWS)]
-        if side == 0:
-            own = pltpu.roll(own, LANES - 1, axis=1)
-            mask = pltpu.roll(mask, LANES - 1, axis=1)
-        wet = spread_mask(mask)
-        col_edges.append((own, wet, pressure_of(own, wet)))
+    column_lane = lane < 2 * ROWS
+    column_sign = jnp.where(lane < ROWS, -1.0, 1.0)
+
+    def row_edge(fields_there, planes):
+        wet = wet_levels(row, *planes)
+        half = half_density(fields_there[0], fields_there[1], wet > 0.5, row_float)
+        return fields_there, wet, half
+
+    def column_edge(buffer, planes):
+        turned = levels_first(*(buffer[side, pl.ds(0, ROWS)] for side in (0, 1)))
+        return row_edge(
+            [turned[n * LEVELS : (n + 1) * LEVELS] for n in range(FIELDS)],
+            [planes[n : n + 1] for n in range(3)],
+        )
+
+    def edge_terms(group, here, there, sign, across, extent=None):
+        own, own_wet, own_half = here
+        other, other_wet, other_half = there
+        face = own_wet * other_wet > 0.5
+        if extent is not None:
+            face = jnp.logical_and(face, extent)
+        a = (sign * FACE) * (own[across] + other[across])
+        for n in range(FIELDS):
+            to = pl.ds(group * FIELDS + n, LEVELS, stride=EDGE)
+            if n < 2:
+                fix = -DIFFUSE * ((a - 1.0) * other[n] + (a + 1.0) * own[n])
+            else:
+                fix = VISCOUS * (other[n] - own[n])
+            edge_value[to] = jnp.where(face, fix * edge_inv[to], 0.0)
+        to = pl.ds(group * FIELDS + across, LEVELS, stride=EDGE)
+        edge_half[to] = other_half - own_half
+        edge_weight[to] = jnp.where(face, (-VISCOUS * sign) * edge_inv[to], 0.0)
+
+    own_rows = [
+        row_edge(
+            [field[pl.ds(edge, LEVELS, stride=ROWS)] for field in fields],
+            [plane[edge : edge + 1] for plane in mask_planes],
+        )
+        for edge in (0, ROWS - 1)
+    ]
+    own_columns = column_edge(col_send, own_planes)
+
+    @pl.when(answers_west)
+    def _():
+        pl.semaphore_wait(go_west, 1)
+        to_west.start()
 
     @pl.when(answers_north)
     def _():
-        from_north.wait_recv()
+        pl.semaphore_wait(go_north, 1)
         to_north.start()
 
-    pl.when(first_north)(from_north.wait_recv)
+    from_north.wait_recv()
     pl.when(lat > 0)(from_south.wait_recv)
-
     for side in (0, 1):
-        own, own_wet, own_p = row_edges[side]
-        other = [row_recv[side, pl.ds(n * LEVELS, LEVELS)] for n in range(FIELDS)]
-        other_wet = wet_levels(
-            row, *(row_recv[side, pl.ds(MASK_ROW + n, 1)] for n in range(3))
-        )
-        other_p = summed(half_density(other[0], other[1], other_wet > 0.5, row_float), 0, row)
-        face = own_wet * other_wet > 0.5
-        sign = 1.0 if side else -1.0
-        a = (sign * FACE) * (own[3] + other[3])
-        fixes = (
-            -DIFFUSE * edge_faces(own[0], other[0], a, face),
-            -DIFFUSE * edge_faces(own[1], other[1], a, face),
-            jnp.where(face, VISCOUS * (other[2] - own[2]), 0.0),
-            jnp.where(face, VISCOUS * ((other[3] - own[3]) - sign * (other_p - own_p)), 0.0),
-        )
-        for n, fix in enumerate(fixes):
-            to = pl.ds(side * FIELDS + n, LEVELS, stride=EDGE)
-            edge_value[to] = fix * edge_inv[to]
+        there = row_edge(
+            [row_recv[side, pl.ds(n * LEVELS, LEVELS)] for n in range(FIELDS)],
+            [row_recv[side, pl.ds(MASK_ROW + n, 1)] for n in range(3)],
+        )
+        edge_terms(side, own_rows[side], there, 1.0 if side else -1.0, 3)
 
     from_east.wait_recv()
-
-    @pl.when(answers_west)
-    def _():
-        from_west.wait_recv()
-        to_west.start()
-
-    pl.when(first_west)(from_west.wait_recv)
-
-    fixes = []
-    for side in (0, 1):
-        own, own_wet, own_p = col_edges[side]
-        other = col_recv[side, pl.ds(0, ROWS)]
-        other_mask = col_recv[side, pl.ds(ROWS, ROWS)]
-        if side == 1:
-            other = pltpu.roll(other, LANES - 1, axis=1)
-            other_mask = pltpu.roll(other_mask, LANES - 1, axis=1)
-        other_wet = spread_mask(other_mask)
-        jump_p = pressure_of(other, other_wet) - own_p
-        face = own_wet * other_wet > 0.5
-        sign = 1.0 if side else -1.0
-        both = own + other
-        a = (sign * FACE) * jnp.where(
-            first_group, pltpu.roll(both, 2 * LEVELS, axis=1), pltpu.roll(both, 3 * LEVELS, axis=1)
-        )
-        tracers = -DIFFUSE * edge_faces(own, other, a, face)
-        jump = other - own
-        jump = jnp.where(
-            lane < 3 * LEVELS, jump - sign * pltpu.roll(jump_p, 2 * LEVELS, axis=1), jump
-        )
-        currents = jnp.where(face, VISCOUS * jump, 0.0)
-        fixes.append(jnp.where(lane < 2 * LEVELS, tracers, currents))
-    turned = side_by_side(*fixes)
-    for n in range(FIELDS):
-        to = pl.ds(2 * FIELDS + n, LEVELS, stride=EDGE)
-        edge_value[to] = turned[n * LEVELS : (n + 1) * LEVELS] * edge_inv[to]
-
-    def edge_level(k):
-        return pl.ds(pl.multiple_of(k * EDGE, EDGE), EDGE)
-
-    def edge_forward(k, value):
-        here = edge_level(k)
-        value = edge_value[here] + edge_down[here] * value
-        edge_value[here] = value
-        return value
-
-    value = lax.fori_loop(
-        0, LEVELS, edge_forward, jnp.zeros((EDGE, LANES), jnp.float32), unroll=8
-    )
-
-    def edge_backward(step, value):
-        here = edge_level(LEVELS - 2 - step)
-        value = edge_value[here] + edge_up[here] * value
-        edge_value[here] = value
-        return value
-
-    lax.fori_loop(0, LEVELS - 1, edge_backward, value, unroll=8)
-
-    for side, edge in ((0, 0), (1, ROWS - 1)):
-        there = pl.ds(edge, LEVELS, stride=ROWS)
-        for n in range(FIELDS):
-            outs[n][there] += edge_value[pl.ds(side * FIELDS + n, LEVELS, stride=EDGE)]
-    for n in range(FIELDS):
-        square[pl.ds(n * LEVELS, LEVELS)] = edge_value[pl.ds(2 * FIELDS + n, LEVELS, stride=EDGE)]
-    turned = square[...].T
+    from_west.wait_recv()
+    planes = jnp.where(
+        lane[:8] < ROWS, col_recv[0, pl.ds(ROWS, 8)], col_recv[1, pl.ds(ROWS, 8)]
+    )
+    edge_terms(2, own_columns, column_edge(col_recv, planes), column_sign, 2, column_lane)
+
+    total = jnp.zeros((EDGE, LANES), jnp.float32)
+    values = []
+    for k in range(LEVELS):
+        half = edge_half[edge_level(k)]
+        total = total + half
+        value = edge_value[edge_level(k)] + edge_weight[edge_level(k)] * total
+        total = total + half
+        if k % BLOCK:
+            value = value + edge_down[edge_level(k)] * values[-1]
+        values.append(value)
+    for start in range(BLOCK, LEVELS, BLOCK):
+        for k in range(start, start + BLOCK):
+            values[k] = values[k] + edge_down_block[edge_level(k)] * values[start - 1]
+    for k in range(LEVELS - 2, -1, -1):
+        if (k + 1) % BLOCK:
+            values[k] = values[k] + edge_up[edge_level(k)] * values[k + 1]
+    for end in range(LEVELS - BLOCK, 0, -BLOCK):
+        for k in range(end - BLOCK, end):
+            values[k] = values[k] + edge_up_block[edge_level(k)] * values[end]
+    for k in range(LEVELS):
+        edge_value[edge_level(k)] = values[k]
+
+    turned = jnp.concatenate(
+        [edge_value[pl.ds(2 * FIELDS + n, LEVELS, stride=EDGE)] for n in range(FIELDS)], axis=0
+    ).T
     west_fix = pltpu.roll(turned[:ROWS], 1, axis=1)
     east_fix = turned[ROWS : 2 * ROWS]
     even_lane = lax.rem(lane, 2) == 0
@@ -600,7 +591,9 @@
         to_south.wait_send()
 
 
-def finish(warm, salt, zonal, merid, col_fix, warm_hbm, salt_hbm, zonal_hbm, merid_hbm, done, sem):
+def finish(
+    warm, salt, zonal, merid, col_fix, edge_value, warm_hbm, salt_hbm, zonal_hbm, merid_hbm, done, sem
+):
     lane = iota(1)
     edge_lane = jnp.logical_or(lane == 0, lane == LANES - 1)
     sources = (warm, salt, zonal, merid)
@@ -613,6 +606,9 @@
             fix = col_fix[pl.ds(k % 2 * ROWS, ROWS)]
             turned = pltpu.roll(fix, LANES - 1 - n * LEVELS - k, axis=1)
             done[n, here] = sources[n][here] + jnp.where(edge_lane, turned, 0.0)
+        for side, edge in ((0, 0), (1, ROWS - 1)):
+            there = pl.ds(edge, LEVELS, stride=ROWS)
+            done[n, there] += edge_value[pl.ds(side * FIELDS + n, LEVELS, stride=EDGE)]
         store = pltpu.make_async_copy(done.at[n], targets[n], sem.at[n])
         store.start()
         stores.append(store)
@@ -640,9 +636,10 @@
             out_shape=[
                 *[result(pltpu.VMEM, CELLS)] * FIELDS,
                 result(pltpu.VMEM, 2 * ROWS),
+                result(pltpu.VMEM, LEVELS * EDGE),
             ],
             in_specs=[pl.BlockSpec(memory_space=pl.ANY)] * 7,
-            out_specs=[pl.BlockSpec(memory_space=pltpu.VMEM)] * (FIELDS + 1),
+            out_specs=[pl.BlockSpec(memory_space=pltpu.VMEM)] * (FIELDS + 2),
             scratch_shapes=[
                 *[pltpu.VMEM((CELLS + 8, LANES), f32)] * FIELDS,
                 pltpu.VMEM((CELLS, LANES), f32),
@@ -653,13 +650,14 @@
                 pltpu.VMEM((CELLS, LANES), f32),
                 pltpu.VMEM((2, MASK_ROW + 8, LANES), f32),
                 pltpu.VMEM((2, MASK_ROW + 8, LANES), f32),
-                pltpu.VMEM((2, 2 * ROWS, LANES), f32),
-                pltpu.VMEM((2, 2 * ROWS, LANES), f32),
-                *[pltpu.VMEM((LEVELS * EDGE, LANES), f32)] * 4,
-                pltpu.VMEM((LANES, LANES), f32),
+                pltpu.VMEM((2, ROWS + 8, LANES), f32),
+                pltpu.VMEM((2, ROWS + 8, LANES), f32),
+                *[pltpu.VMEM((LEVELS * EDGE, LANES), f32)] * 7,
                 pltpu.SemaphoreType.DMA((7,)),
                 pltpu.SemaphoreType.DMA((4,)),
                 pltpu.SemaphoreType.DMA((4,)),
+                pltpu.SemaphoreType.REGULAR,
+                pltpu.SemaphoreType.REGULAR,
             ],
             compiler_params=pltpu.CompilerParams(
                 collective_id=0, has_side_effects=True, vmem_limit_bytes=16 * 1024 * 1024
@@ -668,7 +666,7 @@
         outs = pl.pallas_call(
             finish,
             out_shape=[result(pltpu.HBM, CELLS)] * FIELDS,
-            in_specs=[pl.BlockSpec(memory_space=pltpu.VMEM)] * (FIELDS + 1),
+            in_specs=[pl.BlockSpec(memory_space=pltpu.VMEM)] * (FIELDS + 2),
             out_specs=[pl.BlockSpec(memory_space=pltpu.HBM)] * FIELDS,
             scratch_shapes=[
                 pltpu.VMEM((FIELDS, CELLS, LANES), f32),

time: 20.8 us -> 19.2 us (0.923)
  the two profiles are of different devices: /device:TPU:61 before, /device:TPU:24 now
where the time goes in v3:
time: 19.2 us; the launch traced here: 19 us
  Pallas kernels  18.4 us (96%)
  between operations  0.64 us (3%)
    pallas_call x1, Pallas kernels, step(): pl.pallas_call(functools.partial(kernel, lat_count, lon_count), out_shape...  16.8 us
    pallas_call x1, Pallas kernels, step(): pl.pallas_call(finish, out_shape=[result(pltpu.HBM, CELLS)] * FIELDS, in_...  1.59 us

profile of v3, /device:TPU:24, one launch (start us, length us, event | category | flops | bytes accessed | tf_op | source)
XLA Modules:
  0.0 19.0 jit_solution(17001108707504855786)
XLA Ops:
  0.6 16.8 %shard_map.102 = (f32[1024,128]{1,0:T(8,128)S(1)}, f32[1024,128]{1,0:T(8,128)S(1)}, f32[1024,128]{1,0:T(8,128)S(1)}, f32[1024,128]{1,0:T(8,128)S(1)}, f32[64,128]{1,0:T(8,128)S(1)}, /*index=5*/f32[512,128]{1,0:T(8,128)S(1)}) custom-call(f32[1024,128]{1,0:T(8,128)} %bitcast.10, f32[1024,128]{1,0:T(8,128)} %bitcast.11, f32[1024,128]{1,0:T(8,128)} %bitcast.12, ...), custom_call_target="tpu_custom_call" | custom-call | tf_op jit(solution)/shard_map/pallas_call | solution.py:634
  17.4 1.6 %shard_map.103 = (f32[1024,128]{1,0:T(8,128)}, f32[1024,128]{1,0:T(8,128)}, f32[1024,128]{1,0:T(8,128)}, f32[1024,128]{1,0:T(8,128)}) custom-call(f32[1024,128]{1,0:T(8,128)S(1)} %get-tuple-element.14.warm, f32[1024,128]{1,0:T(8,128)S(1)} %get-tuple-element.15.salt, f32[1024,128]{1,0:T(8,128)S(1)} %get-tuple-element.16.zonal, ...), custom_call_target="tpu_custom_call" | custom-call | tf_op jit(solution)/shard_map/pallas_call | solution.py:666

commit v4 on v3

--- a/solution.py
+++ b/solution.py
@@ -33,6 +33,7 @@
 EDGE = 16
 UNROLL = 3
 BLOCK = 4
+PARTS = 2
 FOLD_TURNS = (0, 1, 3, 5, 0, 0, 0, 0)
 PRESSURE_SCALE = 0.5 / LEVELS * (0.5 * GRADIENT / VISCOUS)
 FACE = 0.25 * ADVECT / DIFFUSE
@@ -600,18 +601,21 @@
     targets = (warm_hbm, salt_hbm, zonal_hbm, merid_hbm)
     stores = []
     for n in range(FIELDS):
-
-        for k in range(LEVELS):
-            here = pl.ds(k * ROWS, ROWS)
-            fix = col_fix[pl.ds(k % 2 * ROWS, ROWS)]
-            turned = pltpu.roll(fix, LANES - 1 - n * LEVELS - k, axis=1)
-            done[n, here] = sources[n][here] + jnp.where(edge_lane, turned, 0.0)
-        for side, edge in ((0, 0), (1, ROWS - 1)):
-            there = pl.ds(edge, LEVELS, stride=ROWS)
-            done[n, there] += edge_value[pl.ds(side * FIELDS + n, LEVELS, stride=EDGE)]
-        store = pltpu.make_async_copy(done.at[n], targets[n], sem.at[n])
-        store.start()
-        stores.append(store)
+        for part in range(PARTS):
+            levels = LEVELS // PARTS
+            first = part * levels
+            for k in range(first, first + levels):
+                here = pl.ds(k * ROWS, ROWS)
+                fix = col_fix[pl.ds(k % 2 * ROWS, ROWS)]
+                turned = pltpu.roll(fix, LANES - 1 - n * LEVELS - k, axis=1)
+                done[n, here] = sources[n][here] + jnp.where(edge_lane, turned, 0.0)
+            for side, edge in ((0, 0), (1, ROWS - 1)):
+                there = pl.ds(first * ROWS + edge, levels, stride=ROWS)
+                done[n, there] += edge_value[pl.ds(first * EDGE + side * FIELDS + n, levels, stride=EDGE)]
+            cells = pl.ds(first * ROWS, levels * ROWS)
+            store = pltpu.make_async_copy(done.at[n, cells], targets[n].at[cells], sem.at[n, part])
+            store.start()
+            stores.append(store)
     for store in stores:
         store.wait()
 
@@ -636,23 +640,23 @@
             out_shape=[
                 *[result(pltpu.VMEM, CELLS)] * FIELDS,
                 result(pltpu.VMEM, 2 * ROWS),
-                result(pltpu.VMEM, LEVELS * EDGE),
+                result(pltpu.VMEM, (LEVELS + 1) * EDGE),
             ],
             in_specs=[pl.BlockSpec(memory_space=pl.ANY)] * 7,
             out_specs=[pl.BlockSpec(memory_space=pltpu.VMEM)] * (FIELDS + 2),
             scratch_shapes=[
-                *[pltpu.VMEM((CELLS + 8, LANES), f32)] * FIELDS,
+                *[pltpu.VMEM((CELLS + ROWS, LANES), f32)] * FIELDS,
                 pltpu.VMEM((CELLS, LANES), f32),
                 pltpu.VMEM((2 * ROWS, LANES), jnp.int32),
                 pltpu.VMEM((ROWS, LANES), jnp.int32),
+                pltpu.VMEM((CELLS + 2 * ROWS, LANES), f32),
                 pltpu.VMEM((CELLS + ROWS, LANES), f32),
-                pltpu.VMEM((CELLS, LANES), f32),
-                pltpu.VMEM((CELLS, LANES), f32),
+                pltpu.VMEM((CELLS + ROWS, LANES), f32),
                 pltpu.VMEM((2, MASK_ROW + 8, LANES), f32),
                 pltpu.VMEM((2, MASK_ROW + 8, LANES), f32),
                 pltpu.VMEM((2, ROWS + 8, LANES), f32),
                 pltpu.VMEM((2, ROWS + 8, LANES), f32),
-                *[pltpu.VMEM((LEVELS * EDGE, LANES), f32)] * 7,
+                *[pltpu.VMEM(((LEVELS + 1) * EDGE, LANES), f32)] * 7,
                 pltpu.SemaphoreType.DMA((7,)),
                 pltpu.SemaphoreType.DMA((4,)),
                 pltpu.SemaphoreType.DMA((4,)),
@@ -669,8 +673,8 @@
             in_specs=[pl.BlockSpec(memory_space=pltpu.VMEM)] * (FIELDS + 2),
             out_specs=[pl.BlockSpec(memory_space=pltpu.HBM)] * FIELDS,
             scratch_shapes=[
-                pltpu.VMEM((FIELDS, CELLS, LANES), f32),
-                pltpu.SemaphoreType.DMA((FIELDS,)),
+                pltpu.VMEM((FIELDS, CELLS + ROWS, LANES), f32),
+                pltpu.SemaphoreType.DMA((FIELDS, PARTS)),
             ],
             compiler_params=pltpu.CompilerParams(vmem_limit_bytes=8 * 1024 * 1024),
         )(*[keep_in(x, pltpu.VMEM) for x in solved])

time: 19.2 us -> 19.2 us (level)
  no operation moved by 1% of the time
where the time goes in v4:
time: 19.2 us; the launch traced here: 19 us
  Pallas kernels  18.3 us (95%)
  between operations  0.64 us (3%)
    pallas_call x1, Pallas kernels, step(): pl.pallas_call(functools.partial(kernel, lat_count, lon_count), out_shape...  16.8 us
    pallas_call x1, Pallas kernels, step(): pl.pallas_call(finish, out_shape=[result(pltpu.HBM, CELLS)] * FIELDS, in_...  1.54 us

profile of v4, /device:TPU:24, one launch (start us, length us, event | category | flops | bytes accessed | tf_op | source)
XLA Modules:
  0.0 19.0 jit_solution(7609667562598919156)
XLA Ops:
  0.6 16.8 %shard_map.102 = (f32[1024,128]{1,0:T(8,128)S(1)}, f32[1024,128]{1,0:T(8,128)S(1)}, f32[1024,128]{1,0:T(8,128)S(1)}, f32[1024,128]{1,0:T(8,128)S(1)}, f32[64,128]{1,0:T(8,128)S(1)}, /*index=5*/f32[528,128]{1,0:T(8,128)S(1)}) custom-call(f32[1024,128]{1,0:T(8,128)} %bitcast.10, f32[1024,128]{1,0:T(8,128)} %bitcast.11, f32[1024,128]{1,0:T(8,128)} %bitcast.12, ...), custom_call_target="tpu_custom_call" | custom-call | tf_op jit(solution)/shard_map/pallas_call | solution.py:638
  17.4 1.5 %shard_map.103 = (f32[1024,128]{1,0:T(8,128)}, f32[1024,128]{1,0:T(8,128)}, f32[1024,128]{1,0:T(8,128)}, f32[1024,128]{1,0:T(8,128)}) custom-call(f32[1024,128]{1,0:T(8,128)S(1)} %get-tuple-element.14.warm, f32[1024,128]{1,0:T(8,128)S(1)} %get-tuple-element.15.salt, f32[1024,128]{1,0:T(8,128)S(1)} %get-tuple-element.16.zonal, ...), custom_call_target="tpu_custom_call" | custom-call | tf_op jit(solution)/shard_map/pallas_call | solution.py:670

commit v5 on v4

--- a/solution.py
+++ b/solution.py
@@ -526,15 +526,15 @@
     ]
     own_columns = column_edge(col_send, own_planes)
 
+    @pl.when(answers_north)
+    def _():
+        pl.semaphore_wait(go_north, 1)
+        to_north.start()
+
     @pl.when(answers_west)
     def _():
         pl.semaphore_wait(go_west, 1)
         to_west.start()
-
-    @pl.when(answers_north)
-    def _():
-        pl.semaphore_wait(go_north, 1)
-        to_north.start()
 
     from_north.wait_recv()
     pl.when(lat > 0)(from_south.wait_recv)

time: 19.2 us -> 19.1 us (level)
  the two profiles are of different devices: /device:TPU:24 before, /device:TPU:125 now
where the time goes in v5:
time: 19.1 us; the launch traced here: 18.9 us
  Pallas kernels  18.2 us (95%)
  between operations  0.64 us (3%)
    pallas_call x1, Pallas kernels, step(): pl.pallas_call(functools.partial(kernel, lat_count, lon_count), out_shape...  16.7 us
    pallas_call x1, Pallas kernels, step(): pl.pallas_call(finish, out_shape=[result(pltpu.HBM, CELLS)] * FIELDS, in_...  1.54 us

profile of v5, /device:TPU:125, one launch (start us, length us, event | category | flops | bytes accessed | tf_op | source)
XLA Modules:
  0.0 18.9 jit_solution(9466890553728491853)
XLA Ops:
  0.6 16.7 %shard_map.102 = (f32[1024,128]{1,0:T(8,128)S(1)}, f32[1024,128]{1,0:T(8,128)S(1)}, f32[1024,128]{1,0:T(8,128)S(1)}, f32[1024,128]{1,0:T(8,128)S(1)}, f32[64,128]{1,0:T(8,128)S(1)}, /*index=5*/f32[528,128]{1,0:T(8,128)S(1)}) custom-call(f32[1024,128]{1,0:T(8,128)} %bitcast.10, f32[1024,128]{1,0:T(8,128)} %bitcast.11, f32[1024,128]{1,0:T(8,128)} %bitcast.12, ...), custom_call_target="tpu_custom_call" | custom-call | tf_op jit(solution)/shard_map/pallas_call | solution.py:638
  17.3 1.5 %shard_map.103 = (f32[1024,128]{1,0:T(8,128)}, f32[1024,128]{1,0:T(8,128)}, f32[1024,128]{1,0:T(8,128)}, f32[1024,128]{1,0:T(8,128)}) custom-call(f32[1024,128]{1,0:T(8,128)S(1)} %get-tuple-element.14.warm, f32[1024,128]{1,0:T(8,128)S(1)} %get-tuple-element.15.salt, f32[1024,128]{1,0:T(8,128)S(1)} %get-tuple-element.16.zonal, ...), custom_call_target="tpu_custom_call" | custom-call | tf_op jit(solution)/shard_map/pallas_call | solution.py:670

commit v6 on v5

--- a/solution.py
+++ b/solution.py
@@ -34,7 +34,7 @@
 UNROLL = 3
 BLOCK = 4
 PARTS = 2
-FOLD_TURNS = (0, 1, 3, 5, 0, 0, 0, 0)
+FOLD_TURNS = (0, 1, 3, 4, 0, 0, 0, 0)
 PRESSURE_SCALE = 0.5 / LEVELS * (0.5 * GRADIENT / VISCOUS)
 FACE = 0.25 * ADVECT / DIFFUSE
 
@@ -104,6 +104,7 @@
     send_sem,
     recv_sem,
     go_west,
+    go_east,
     go_north,
 ):
     lat = lax.axis_index("lat")
@@ -123,7 +124,11 @@
     place = lax.rem(lon, span)
     is_last = place == span - 1
     lat_odd = lax.rem(lat, 2) == 1
-    answers_west = jnp.logical_or(place == 0, is_last)
+    answers_east = jnp.logical_and(is_north, place == span - 4)
+    answers_west = jnp.logical_or(jnp.logical_or(place == 0, is_last), answers_east)
+    before_far = jnp.logical_and(is_north, place == span - 5)
+    after_far = jnp.logical_and(is_north, place == span - 3)
+    first_east = jnp.logical_not(answers_east)
     fold_late = jnp.logical_and(is_north, place >= span // 2)
     answers_north = jnp.logical_and(lat_odd, jnp.logical_not(fold_late))
     first_west = jnp.logical_not(answers_west)
@@ -136,10 +141,10 @@
 
     pl.when(jnp.logical_not(fold_late))(lambda: greet(north))
     pl.when(lat_odd)(lambda: greet(south))
-    pl.when(place < span - 2)(lambda: greet(east))
-    greet(west)
+    pl.when(jnp.logical_and(place < span - 2, jnp.logical_not(before_far)))(lambda: greet(east))
+    pl.when(jnp.logical_not(after_far))(lambda: greet(west))
     greetings = (
-        1
+        jnp.where(first_east, 1, 0)
         + jnp.where(first_west, 1, 0)
         + jnp.where(first_north, 1, 0)
         + jnp.where(is_south, 0, 1)
@@ -153,7 +158,8 @@
         def go(sem, target):
             pl.semaphore_signal(sem, inc=1, device_id=target, device_id_type=MESH)
 
-        pl.when(place >= span - 2)(lambda: go(go_west, east))
+        pl.when(jnp.logical_or(place >= span - 2, before_far))(lambda: go(go_west, east))
+        pl.when(after_far)(lambda: go(go_east, west))
         pl.when(jnp.logical_and(jnp.logical_not(lat_odd), lat > 0))(lambda: go(go_north, south))
         pl.when(fold_late)(lambda: go(go_north, north))
 
@@ -280,7 +286,7 @@
     north_turn = 0
     for n, turn in enumerate(FOLD_TURNS):
         north_turn = jnp.where(jnp.logical_and(fold_late, place == span - 1 - n), turn, north_turn)
-    to_east.start()
+    pl.when(first_east)(to_east.start)
     pl.when(first_west)(to_west.start)
     pl.when(jnp.logical_and(first_north, north_turn == 0))(to_north.start)
     pl.when(lat > 0)(to_south.start)
@@ -530,6 +536,11 @@
     def _():
         pl.semaphore_wait(go_north, 1)
         to_north.start()
+
+    @pl.when(answers_east)
+    def _():
+        pl.semaphore_wait(go_east, 1)
+        to_east.start()
 
     @pl.when(answers_west)
     def _():
@@ -662,6 +673,7 @@
                 pltpu.SemaphoreType.DMA((4,)),
                 pltpu.SemaphoreType.REGULAR,
                 pltpu.SemaphoreType.REGULAR,
+                pltpu.SemaphoreType.REGULAR,
             ],
             compiler_params=pltpu.CompilerParams(
                 collective_id=0, has_side_effects=True, vmem_limit_bytes=16 * 1024 * 1024

time: 19.1 us -> 18.9 us (0.990)
  Pallas kernels: 18.2 us -> 18 us
where the time goes in v6:
time: 18.9 us; the launch traced here: 18.7 us
  Pallas kernels  18 us (95%)
  between operations  0.64 us (3%)
    pallas_call x1, Pallas kernels, step(): pl.pallas_call(functools.partial(kernel, lat_count, lon_count), out_shape...  16.5 us
    pallas_call x1, Pallas kernels, step(): pl.pallas_call(finish, out_shape=[result(pltpu.HBM, CELLS)] * FIELDS, in_...  1.54 us

profile of v6, /device:TPU:125, one launch (start us, length us, event | category | flops | bytes accessed | tf_op | source)
XLA Modules:
  0.0 18.7 jit_solution(16822941812749940971)
XLA Ops:
  0.6 16.5 %shard_map.102 = (f32[1024,128]{1,0:T(8,128)S(1)}, f32[1024,128]{1,0:T(8,128)S(1)}, f32[1024,128]{1,0:T(8,128)S(1)}, f32[1024,128]{1,0:T(8,128)S(1)}, f32[64,128]{1,0:T(8,128)S(1)}, /*index=5*/f32[528,128]{1,0:T(8,128)S(1)}) custom-call(f32[1024,128]{1,0:T(8,128)} %bitcast.10, f32[1024,128]{1,0:T(8,128)} %bitcast.11, f32[1024,128]{1,0:T(8,128)} %bitcast.12, ...), custom_call_target="tpu_custom_call" | custom-call | tf_op jit(solution)/shard_map/pallas_call | solution.py:649
  17.1 1.5 %shard_map.103 = (f32[1024,128]{1,0:T(8,128)}, f32[1024,128]{1,0:T(8,128)}, f32[1024,128]{1,0:T(8,128)}, f32[1024,128]{1,0:T(8,128)}) custom-call(f32[1024,128]{1,0:T(8,128)S(1)} %get-tuple-element.14.warm, f32[1024,128]{1,0:T(8,128)S(1)} %get-tuple-element.15.salt, f32[1024,128]{1,0:T(8,128)S(1)} %get-tuple-element.16.zonal, ...), custom_call_target="tpu_custom_call" | custom-call | tf_op jit(solution)/shard_map/pallas_call | solution.py:682

commit v7 on v5

--- a/solution.py
+++ b/solution.py
@@ -536,6 +536,13 @@
         pl.semaphore_wait(go_west, 1)
         to_west.start()
 
+    from_east.wait_recv()
+    from_west.wait_recv()
+    planes = jnp.where(
+        lane[:8] < ROWS, col_recv[0, pl.ds(ROWS, 8)], col_recv[1, pl.ds(ROWS, 8)]
+    )
+    edge_terms(2, own_columns, column_edge(col_recv, planes), column_sign, 2, column_lane)
+
     from_north.wait_recv()
     pl.when(lat > 0)(from_south.wait_recv)
     for side in (0, 1):
@@ -544,13 +551,6 @@
             [row_recv[side, pl.ds(MASK_ROW + n, 1)] for n in range(3)],
         )
         edge_terms(side, own_rows[side], there, 1.0 if side else -1.0, 3)
-
-    from_east.wait_recv()
-    from_west.wait_recv()
-    planes = jnp.where(
-        lane[:8] < ROWS, col_recv[0, pl.ds(ROWS, 8)], col_recv[1, pl.ds(ROWS, 8)]
-    )
-    edge_terms(2, own_columns, column_edge(col_recv, planes), column_sign, 2, column_lane)
 
     total = jnp.zeros((EDGE, LANES), jnp.float32)
     values = []

time: 19.1 us -> 18.9 us (0.990)
  Pallas kernels: 18.2 us -> 18 us
    pallas_call x1, Pallas kernels: 16.7 us -> 16.5 us  [step(): pl.pallas_call(functools.partial(kernel, lat_count, lon_count), out_shape...]
where the time goes in v7:
time: 18.9 us; the launch traced here: 18.6 us
  Pallas kernels  18 us (95%)
  between operations  0.64 us (3%)
    pallas_call x1, Pallas kernels, step(): pl.pallas_call(functools.partial(kernel, lat_count, lon_count), out_shape...  16.5 us
    pallas_call x1, Pallas kernels, step(): pl.pallas_call(finish, out_shape=[result(pltpu.HBM, CELLS)] * FIELDS, in_...  1.54 us

profile of v7, /device:TPU:125, one launch (start us, length us, event | category | flops | bytes accessed | tf_op | source)
XLA Modules:
  0.0 18.6 jit_solution(4473845854450124358)
XLA Ops:
  0.6 16.5 %shard_map.102 = (f32[1024,128]{1,0:T(8,128)S(1)}, f32[1024,128]{1,0:T(8,128)S(1)}, f32[1024,128]{1,0:T(8,128)S(1)}, f32[1024,128]{1,0:T(8,128)S(1)}, f32[64,128]{1,0:T(8,128)S(1)}, /*index=5*/f32[528,128]{1,0:T(8,128)S(1)}) custom-call(f32[1024,128]{1,0:T(8,128)} %bitcast.10, f32[1024,128]{1,0:T(8,128)} %bitcast.11, f32[1024,128]{1,0:T(8,128)} %bitcast.12, ...), custom_call_target="tpu_custom_call" | custom-call | tf_op jit(solution)/shard_map/pallas_call | solution.py:638
  17.1 1.5 %shard_map.103 = (f32[1024,128]{1,0:T(8,128)}, f32[1024,128]{1,0:T(8,128)}, f32[1024,128]{1,0:T(8,128)}, f32[1024,128]{1,0:T(8,128)}) custom-call(f32[1024,128]{1,0:T(8,128)S(1)} %get-tuple-element.14.warm, f32[1024,128]{1,0:T(8,128)S(1)} %get-tuple-element.15.salt, f32[1024,128]{1,0:T(8,128)S(1)} %get-tuple-element.16.zonal, ...), custom_call_target="tpu_custom_call" | custom-call | tf_op jit(solution)/shard_map/pallas_call | solution.py:670
